TPU v7x, 512 devices: a whole 4x4x16 slice. The times are simulated.
512 devices in a mesh: corpus: 128 (over z, y, core), query: 4 (over x).
Axes of the slice: x: 4, y: 4, z: 16, core: 2. Of those that a mesh axis runs over, the one named last changes fastest.
Arguments:
- prefixes: bfloat16 [32768, 256], P(('corpus', 'query')), as said below
- tails: bfloat16 [32768, 2816], P('corpus'), as said below
- queries_now: bfloat16 [32768, 256], P(('corpus', 'query')), as said below
- queries_prev: bfloat16 [512, 3072], P(('corpus', 'query')), may hold values from -6 to 6
- candidates: int32 [512, 100], P(('corpus', 'query')), may hold values from 0 to 32767, as said below
- lse_prev: float32 [512], P(('corpus', 'query')), may hold values from 9 to 14
Outputs:
- lse_now: float32 [32768], P(('corpus', 'query'))
- rerank: float32 [512, 100], P(('corpus', 'query'))
Inputs may be any that keep to these rules, and one draw needn't show every extreme that they name: `prefixes`: prefix coordinates of the passage embeddings. `tails`: remaining coordinates of the passage embeddings. `queries_now`: query prefixes. `candidates`: passage j belongs to corpus index j // 256. Among the 100 ids of one device's queries, at most 2 belong to one corpus index, and exactly 2 to some corpus index. Ids may repeat.
All inputs are finite; a program needn't handle non-finite values.
Results may differ from a plain program's by a relative error of at most 0.0003.
Values may be sent and summed in bfloat16 or wider, within the bound.
No kernel may reach another device: no remote copies, remote signals or barrier semaphores. Data moves between devices by JAX's collectives and lax.ppermute only.
A program may use at most 64 MiB of HBM per device.

v0:
```python
import math

import jax
import jax.numpy as jnp
from jax import lax
from jax.sharding import PartitionSpec as P


def merged(part, axis, combine):
    gathered = jax.tree.map(lambda a: lax.all_gather(a, axis), part)

    def take(source):
        return jax.tree.map(lambda a: lax.dynamic_index_in_dim(a, source, 0, False), gathered)

    return lax.fori_loop(
        1, lax.axis_size(axis), lambda source, state: combine(state, take(source)), take(0)
    )


def shard_parts(shard_rows, prefix_rows, scale_pre):
    row_count = shard_rows.shape[0]
    block_size = math.gcd(row_count, 512)

    def score_block(block_rows):
        scores = (
            lax.dot_general(
                block_rows,
                prefix_rows,
                (((1,), (1,)), ((), ())),
                preferred_element_type=jnp.float32,
            )
            * scale_pre
        )
        row_top = jnp.max(scores, axis=1)
        row_sum = jnp.sum(jnp.exp(scores - row_top[:, None]), axis=1)
        return (row_top, row_sum)

    block_tops, block_sums = lax.map(
        score_block, shard_rows.reshape(row_count // block_size, block_size, shard_rows.shape[1])
    )
    return (block_tops.reshape(-1), block_sums.reshape(-1))


def combine_parts(first_part, second_part):
    highest = jnp.maximum(first_part[0], second_part[0])
    totals = first_part[1] * jnp.exp(first_part[0] - highest) + second_part[1] * jnp.exp(
        second_part[0] - highest
    )
    return (highest, totals)


def local(prefixes, tails, queries_now, queries_prev, candidates, lse_prev):
    corpus_count = lax.axis_size("corpus")
    width_pre = queries_now.shape[1]
    full_width = width_pre + tails.shape[1]
    scale_pre = width_pre ** (-0.5)
    prefix_rows = lax.all_gather(prefixes, "query", axis=0, tiled=True)
    pass_count = prefix_rows.shape[0]
    own_rows = queries_now.shape[0]
    part_tops, part_sums = shard_parts(
        lax.all_gather(queries_now, "corpus", axis=0, tiled=True), prefix_rows, scale_pre
    )
    row_peaks = part_tops
    totals = part_sums
    own_start = lax.axis_index("corpus") * own_rows
    row_peaks, totals = merged((row_peaks, totals), "corpus", combine_parts)
    own_peaks = lax.dynamic_slice_in_dim(row_peaks, own_start, own_rows, 0)
    own_sums = lax.dynamic_slice_in_dim(totals, own_start, own_rows, 0)
    lse_now = own_peaks + jnp.log(own_sums)
    per_query = candidates.shape[1]
    query_rows = queries_prev.shape[0]
    flat_ids = candidates.reshape(-1)
    slot_count = flat_ids.shape[0]
    capacity = 2 * ((slot_count + corpus_count - 1) // corpus_count)
    owners = flat_ids // pass_count
    offsets = flat_ids % pass_count
    one_hot = (owners[:, None] == jnp.arange(corpus_count)[None, :]).astype(jnp.float32)
    earlier_mask = (jnp.arange(slot_count)[:, None] > jnp.arange(slot_count)[None, :]).astype(
        jnp.float32
    )
    earlier_counts = jnp.dot(earlier_mask, one_hot, precision=lax.Precision.HIGHEST)
    slots = jnp.sum(earlier_counts * one_hot, axis=1).astype(jnp.int32)
    places = owners * capacity + slots
    query_head = queries_prev[:, :width_pre]
    query_tail = queries_prev[:, width_pre:]
    request_ids = (
        jnp.zeros((corpus_count * capacity,), jnp.int32)
        .at[places]
        .set(offsets)
        .reshape(corpus_count, capacity)
    )
    asked_ids = lax.all_to_all(
        request_ids, "corpus", split_axis=0, concat_axis=0, tiled=True
    ).reshape(-1)
    head_rows = prefix_rows[asked_ids].reshape(corpus_count, capacity, width_pre)
    tail_rows = tails[asked_ids].reshape(corpus_count, capacity, full_width - width_pre)
    head_back, tail_back = (
        lax.all_to_all(head_rows, "corpus", split_axis=0, concat_axis=0, tiled=True),
        lax.all_to_all(tail_rows, "corpus", split_axis=0, concat_axis=0, tiled=True),
    )
    head_picked = head_back.reshape(corpus_count * capacity, width_pre)[places].reshape(
        query_rows, per_query, width_pre
    )
    tail_picked = tail_back.reshape(corpus_count * capacity, full_width - width_pre)[
        places
    ].reshape(query_rows, per_query, full_width - width_pre)
    full_scores = jnp.einsum(
        "qf,qcf->qc", query_head, head_picked, preferred_element_type=jnp.float32
    ) + jnp.einsum("qf,qcf->qc", query_tail, tail_picked, preferred_element_type=jnp.float32)
    rerank = full_scores * full_width ** (-0.5) - lse_prev[:, None]
    return (lse_now, rerank)


def solution(mesh):
    placed = (
        P(("corpus", "query"), None),
        P("corpus", None),
        P(("corpus", "query"), None),
        P(("corpus", "query"), None),
        P(("corpus", "query"), None),
        P(("corpus", "query")),
    )
    return jax.shard_map(
        local,
        mesh=mesh,
        in_specs=placed,
        out_specs=(P(("corpus", "query")), P(("corpus", "query"), None)),
        check_vma=False,
    )
```

profile of v0, /device:TPU:1, one launch (start us, length us, event | category | flops | bytes accessed | tf_op | source)
XLA Modules:
  0.0 636.4 jit_solution(9523250430884660408)
XLA Ops:
  8.0 10.5 %all_gather.13 = bf16[256,256]{1,0:T(8,128)(2,1)S(1)} all-gather(bf16[64,256]{1,0:T(8,128)(2,1)} %param.10), channel_id=1, replica_groups=mesh['corpus'=128,'query'=4] {'query'}, dimensions={0}, use_global_device_ids=true | all-gather | bytes 163840 | tf_op jit(solution)/shard_map/all_gather | solution.py:57
  18.5 140.4 %all-gather.6.cloned.1.call-done = bf16[8192,256]{1,0:T(8,128)(2,1)} async-done(((bf16[64,256]{1,0:T(8,128)(2,1)}), bf16[8192,256]{1,0:T(8,128)(2,1)}) %all-gather.6.cloned.1.call-update) | async-done | bytes 4194320 | tf_op jit(solution)/shard_map/all_gather | solution.py:61
  158.9 23.8 %while.29 = (s32[]{:T(128)}, f32[16,512]{1,0:T(8,128)S(1)}, f32[16,512]{1,0:T(8,128)S(1)}, bf16[16,512,256]{2,1,0:T(8,128)(2,1)}, bf16[256,256]{1,0:T(8,128)(2,1)S(1)}, /*index=5*/s32[]{:T(128)}, s32[]{:T(128)}) while((s32[]{:T(128)}, f32[16,512]{1,0:T(8,128)S(1)}, f32[16,512]{1,0:T(8,128)S(1)}, bf16[16,512,256]{2,1,0:T(8,128)(2,1)}, ...), condition=%wide.region_3.4_spmd, body=%wide.region_0.3_spmd.sunk | while | flops 67632128 | bytes 1456225 | solution.py:38
  158.9 1.2 fusion.23
  161.9 1.2 fusion.23
  164.9 1.2 fusion.23
  167.9 1.2 fusion.23
  170.8 1.2 fusion.23
  173.8 1.2 fusion.23
  176.8 1.2 fusion.23
  179.8 1.2 fusion.23
  185.6 25.5 %all_to_all.19 = s32[128,1,2]{2,1,0:T(1,128)S(1)} all-to-all(s32[128,1,2]{2,1,0:T(1,128)S(1)} %bitcast.96), channel_id=1, replica_groups=mesh['corpus'=128,'query'=4] {'corpus'}, dimensions={0} | all-to-all | bytes 2048 | tf_op jit(solution)/shard_map/all_to_all | solution.py:92
  214.4 5.7 all-to-all-start.1
  220.2 1.5 gather_fusion.2
  221.7 1.5 reshape.190
  223.2 13.3 %all-to-all-done.1 = bf16[128,2,256]{2,1,0:T(2,128)(2,1)S(1)} async-done(((bf16[128,2,256]{2,1,0:T(2,128)(2,1)}), bf16[128,2,256]{2,1,0:T(2,128)(2,1)S(1)}, u32[]{:S(2)}, u32[]{:S(2)}) %all-to-all-start.1) | async-done | bytes 131104 | tf_op jit(solution)/shard_map/all_to_all | solution.py:98
  236.5 7.6 %all-to-all-start.2 = ((bf16[128,2,2816]{2,1,0:T(2,128)(2,1)}), bf16[128,2,2816]{2,1,0:T(2,128)(2,1)}, u32[]{:S(2)}, u32[]{:S(2)}) async-start(bf16[128,2,2816]{2,1,0:T(2,128)(2,1)} %reshape.190), calls=%async_computation.2 | async-start | bytes 2883584 | tf_op jit(solution)/shard_map/all_to_all | solution.py:99
  245.7 72.8 %all-to-all-done.2 = bf16[128,2,2816]{2,1,0:T(2,128)(2,1)} async-done(((bf16[128,2,2816]{2,1,0:T(2,128)(2,1)}), bf16[128,2,2816]{2,1,0:T(2,128)(2,1)}, u32[]{:S(2)}, u32[]{:S(2)}) %all-to-all-start.2) | async-done | bytes 1441824 | tf_op jit(solution)/shard_map/all_to_all | solution.py:99
  318.5 3.4 reshape.191
  323.8 10.3 %all-gather.8.cloned.1.call-done = f32[128,1,8192]{2,1,0:T(1,128)} async-done(((f32[1,1,8192]{2,1,0:T(1,128)}), f32[128,1,8192]{2,1,0:T(1,128)}) %all-gather.8.cloned.1.call-update) | async-done | bytes 4194320 | tf_op jit(solution)/shard_map/all_gather | solution.py:10
  334.0 7.4 %copy.14 = f32[128,1,8192]{2,0,1:T(8,128)} copy(f32[128,1,8192]{2,1,0:T(1,128)} %all-gather.8.cloned.1.call-done) | data formatting | bytes 8388608
  341.4 135.0 %all-gather.10.cloned.1.call-done = f32[128,1,8192]{2,1,0:T(1,128)} async-done(((f32[1,1,8192]{2,1,0:T(1,128)}), f32[128,1,8192]{2,1,0:T(1,128)}) %all-gather.10.cloned.1.call-update) | async-done | bytes 4194320 | tf_op jit(solution)/shard_map/all_gather | solution.py:10
  476.5 7.5 %copy.13 = f32[128,1,8192]{2,0,1:T(8,128)} copy(f32[128,1,8192]{2,1,0:T(1,128)} %all-gather.10.cloned.1.call-done) | data formatting | bytes 8388608
  483.9 145.4 %while.30 = (s32[]{:T(128)}, f32[8192]{0:T(1024)S(1)}, f32[8192]{0:T(1024)S(1)}, f32[128,8192]{1,0:T(8,128)}, f32[128,8192]{1,0:T(8,128)}, /*index=5*/s32[]{:T(128)}, s32[]{:T(128)}, s32[]{:T(128)}) while((s32[]{:T(128)}, f32[8192]{0:T(1024)S(1)}, f32[8192]{0:T(1024)S(1)}, f32[128,8192]{1,0:T(8,128)}, f32[128,8192]{1,0:T(8,128)}, ...), condition=%wide.region_5.6_spmd, body=%wide.region_4.5_spmd.sunk | while | flops 49157 | bytes 327811 | solution.py:15
  (349 shorter events, 165.9 us)
Async XLA Ops:
  7.2 213.0 %copy-start = (bf16[256,2816]{1,0:T(8,128)(2,1)S(1)}, bf16[256,2816]{1,0:T(8,128)(2,1)}, u32[]{:S(2)}) copy-start(bf16[256,2816]{1,0:T(8,128)(2,1)} %param.11) | copy-start | bytes 4325380
  7.2 151.7 %all-gather.6.cloned.1.call-start = ((), (), s32[]{:S(2)}) async-start(), calls=%async_computation.3 | async-start | bytes 4227072 | tf_op jit(solution)/shard_map/all_gather | solution.py:61
  7.9 326.1 %all-gather.8.cloned.1.call-start = ((), (), s32[]{:S(2)}) async-start(), calls=%async_computation.4 | async-start | bytes 4227072 | tf_op jit(solution)/shard_map/all_gather | solution.py:10
  158.9 25.3 %copy-start.2 = (s32[1,100]{1,0:T(1,128)S(1)}, s32[1,100]{1,0:T(1,128)}, u32[]{:S(2)}) copy-start(s32[1,100]{1,0:T(1,128)} %param.14) | copy-start | bytes 1204
  183.4 293.0 %all-gather.10.cloned.1.call-start = ((), (), s32[]{:S(2)}) async-start(), calls=%async_computation.5 | async-start | bytes 4227072 | tf_op jit(solution)/shard_map/all_gather | solution.py:10
  214.4 22.1 %all-to-all-start.1 = ((bf16[128,2,256]{2,1,0:T(2,128)(2,1)}), bf16[128,2,256]{2,1,0:T(2,128)(2,1)S(1)}, u32[]{:S(2)}, u32[]{:S(2)}) async-start(bf16[128,2,256]{2,1,0:T(2,128)(2,1)} %reshape.187), calls=%async_computation.1 | async-start | bytes 262144 | tf_op jit(solution)/shard_map/all_to_all | solution.py:98
  236.5 82.0 %all-to-all-start.2 = ((bf16[128,2,2816]{2,1,0:T(2,128)(2,1)}), bf16[128,2,2816]{2,1,0:T(2,128)(2,1)}, u32[]{:S(2)}, u32[]{:S(2)}) async-start(bf16[128,2,2816]{2,1,0:T(2,128)(2,1)} %reshape.190), calls=%async_computation.2 | async-start | bytes 2883584 | tf_op jit(solution)/shard_map/all_to_all | solution.py:99
  321.9 0.9 copy-start.1
  476.5 7.5 %slice-start = ((f32[128,1,8192]{2,1,0:T(1,128)}), f32[1,1,8192]{2,1,0:T(1,128)S(1)}, s32[]{:S(2)}) async-start(f32[128,1,8192]{2,1,0:T(1,128)} %all-gather.8.cloned.1.call-done), calls=%async_computation.6 | async-start | bytes 65536 | tf_op jit(solution)/shard_map/jit(dynamic_index_in_dim)/dynamic_slice | solution.py:13
  476.5 7.5 %slice-start.1 = ((f32[128,1,8192]{2,1,0:T(1,128)}), f32[1,1,8192]{2,1,0:T(1,128)S(1)}, s32[]{:S(2)}) async-start(f32[128,1,8192]{2,1,0:T(1,128)} %all-gather.10.cloned.1.call-done), calls=%async_computation.7 | async-start | bytes 65536 | tf_op jit(solution)/shard_map/jit(dynamic_index_in_dim)/dynamic_slice | solution.py:13
Sparse Core Ops, SparseCore 0:
  11.2 147.7 all-gather.5
  183.6 150.4 all-gather.7
  337.2 139.2 all-gather.9
where the time goes:
time: 640 us; the launch traced here: 636 us
  waiting for transfers between devices  373 us (58%)
  local copies, waits for them, and re-layouts  167 us (26%)
  blocking collectives  36 us (6%)
  matrix products  20.9 us (3%)
  between operations  14.6 us (2%)
  starting transfers between devices  13.5 us (2%)
  other arithmetic  8.1 us (1%)
    all_gather x2, waiting for transfers between devices, merged(): gathered = jax.tree.map(lambda a: lax.all_gather(a, axis), part)  145 us
    all_gather x1, waiting for transfers between devices, local(): lax.all_gather(queries_now, 'corpus', axis=0, tiled=True)  140 us
    dynamic_slice x131, local copies, waits for them, and re-layouts, take(): lax.dynamic_index_in_dim(a, source, 0, False)  137 us
    all_to_all x1, waiting for transfers between devices, local(): lax.all_to_all(tail_rows, 'corpus', split_axis=0, concat_axis=0, tiled=True)  72.8 us
    all_to_all x1, blocking collectives, local(): lax.all_to_all(request_ids, 'corpus', split_axis=0, concat_axis=0, tiled=...  25.5 us
    dot_general x16, matrix products, score_block(): lax.dot_general(block_rows, prefix_rows, (((1,), (1,)), ((), ())), prefer...  19.6 us
    unnamed x10, local copies, waits for them, and re-layouts  16.2 us
    all_to_all x1, waiting for transfers between devices, local(): lax.all_to_all(head_rows, 'corpus', split_axis=0, concat_axis=0, tiled=True)  13.3 us
  transfers between devices with their start and end apart: 5, of which 5 were waited for; matrix products, arithmetic and copies ran while one was open for 3% of the time, Pallas kernels for 0%

commit v1 on v0

v1 whole, which is shorter than its diff:
```python
import jax
import jax.numpy as jnp
from jax import lax
from jax.experimental import pallas as pl
from jax.experimental.pallas import tpu as pltpu
from jax.sharding import Mesh, PartitionSpec as P

ALL = ("z", "y", "core", "x")
PLANE = ("y", "core", "x")
BACK = ("core", "y", "z")
LOG2E = 1.4426950408889634


def partial_lse(scale, queries_ref, passages_ref, out_ref, scores):
    groups, rows = queries_ref.shape[0], out_ref.shape[1] // queries_ref.shape[0]
    width = passages_ref.shape[1]
    block = queries_ref[:, :rows, :].reshape(groups * rows, width)
    count, step = passages_ref.shape[0], 256
    top = None
    for start in range(0, count, step):
        part = lax.dot_general(
            passages_ref[start : start + step, :],
            block,
            (((1,), (1,)), ((), ())),
            preferred_element_type=jnp.float32,
        )
        scores[start : start + step, :] = part
        high = jnp.max(part.reshape(step // 8, 8, groups * rows), axis=0)
        top = high if top is None else jnp.maximum(top, high)
    peak = jnp.max(top, axis=0, keepdims=True)
    total = None
    for start in range(0, count, step):
        part = jnp.exp2((scores[start : start + step, :] - peak) * (scale * LOG2E))
        added = jnp.sum(part.reshape(step // 8, 8, groups * rows), axis=0)
        total = added if total is None else total + added
    out_ref[...] = peak * scale + jnp.log(jnp.sum(total, axis=0, keepdims=True))


def passage_scores(place_ref, asked_ref, prefixes_ref, tails_ref, out_ref):
    rows, head = tails_ref.shape[0], prefixes_ref.shape[1]
    start = pl.multiple_of(place_ref[0] * rows, rows)
    dims = (((1,), (1,)), ((), ()))
    out_ref[...] = lax.dot_general(
        asked_ref[:, :head], prefixes_ref[pl.ds(start, rows), :], dims, preferred_element_type=jnp.float32
    ) + lax.dot_general(asked_ref[:, head:], tails_ref[...], dims, preferred_element_type=jnp.float32)


def finish(scale, rows, own_ref, row_ref, column_ref, back_ref, prev_ref, lse_ref, rerank_ref, picked):
    count = rerank_ref.shape[1]
    width = back_ref.shape[1]
    depth = 16
    start = pl.multiple_of(own_ref[0] * depth, depth)
    parts = back_ref[pl.ds(start, depth), rows:]
    peak = jnp.max(parts, axis=0, keepdims=True)
    lse_ref[...] = peak + jnp.log(jnp.sum(jnp.exp(parts - peak), axis=0, keepdims=True))
    lanes = lax.broadcasted_iota(jnp.int32, (1, rows), 1)
    picked[...] = jnp.zeros_like(picked)
    for k in range(count):
        row = back_ref[pl.ds(row_ref[k], 1), :rows]
        row = jnp.where(lanes == column_ref[k], row, 0.0)
        picked[k : k + 1, :] = row[:, :128] + row[:, 128:]
    values = jnp.sum(picked[...].T, axis=0, keepdims=True)
    rerank_ref[...] = values[:, :count] * scale - prev_ref[0]


def local(prefixes, tails, queries_now, queries_prev, candidates, lse_prev):
    vmem, smem = pl.BlockSpec(memory_space=pltpu.VMEM), pl.BlockSpec(memory_space=pltpu.SMEM)
    depth = lax.axis_size("z")
    own_rows, head = queries_now.shape
    shard_rows = tails.shape[0]
    full_width = queries_prev.shape[1]
    plane = lax.axis_size("y") * lax.axis_size("core")

    passages = lax.all_to_all(
        jnp.broadcast_to(prefixes[None], (plane * lax.axis_size("x"),) + prefixes.shape),
        PLANE, 0, 0, tiled=True,
    ).reshape(-1, head)

    extra = full_width // head
    sent = jnp.concatenate([queries_now, queries_prev.reshape(extra, head), jnp.zeros((16 - extra, head), queries_now.dtype)])
    column = lax.all_gather(sent, "z")
    asked = column[:, own_rows : own_rows + extra].reshape(depth, full_width)

    asked = lax.all_to_all(
        jnp.broadcast_to(asked[None], (lax.axis_size("y"),) + asked.shape), "y", 0, 0, tiled=True
    ).reshape(-1, full_width)
    asked = lax.all_gather(asked, "core", tiled=True)

    step = 4
    lse_parts = pl.pallas_call(
        lambda *refs: partial_lse(head**-0.5, *refs),
        grid=(depth // step,),
        in_specs=[
            pl.BlockSpec((step,) + column.shape[1:], lambda i: (i, 0, 0)),
            pl.BlockSpec(passages.shape, lambda i: (0, 0)),
        ],
        out_specs=pl.BlockSpec((1, step * own_rows), lambda i: (0, i)),
        out_shape=jax.ShapeDtypeStruct((1, depth * own_rows), jnp.float32),
        scratch_shapes=[pltpu.VMEM((passages.shape[0], step * own_rows), jnp.float32)],
        compiler_params=pltpu.CompilerParams(vmem_limit_bytes=32 * 2**20),
        cost_estimate=pl.CostEstimate(flops=2 * 2**28, bytes_accessed=2 * 2**20, transcendentals=2**21),
        name="partial_lse",
    )(column, passages)

    place = lax.axis_index("y") * lax.axis_size("core") + lax.axis_index("core")
    scores = pl.pallas_call(
        passage_scores,
        in_specs=[smem, vmem, vmem, vmem],
        out_specs=vmem,
        out_shape=jax.ShapeDtypeStruct((plane * depth, shard_rows), jnp.float32),
        compiler_params=pltpu.CompilerParams(vmem_limit_bytes=32 * 2**20),
        cost_estimate=pl.CostEstimate(flops=2 * 128 * 256 * 3072, bytes_accessed=3 * 2**20, transcendentals=0),
        name="passage_scores",
    )(place.reshape(1), asked, passages, tails)

    merged = jnp.concatenate(
        [scores, jnp.tile(lse_parts.reshape(depth, own_rows), (plane, 1))], axis=1
    )
    back = lax.all_to_all(merged, BACK, 0, 0, tiled=True)

    ids = candidates.reshape(-1)
    shard, offset = ids // shard_rows, ids % shard_rows
    cores, ys = lax.axis_size("core"), lax.axis_size("y")
    row = (shard % cores) * (ys * depth) + (shard // cores % ys) * depth + shard // (cores * ys)
    own = lax.axis_index("core") * ys + lax.axis_index("y")
    lse_now, rerank = pl.pallas_call(
        lambda *refs: finish(full_width**-0.5, shard_rows, *refs),
        in_specs=[smem, smem, smem, vmem, smem],
        out_specs=[vmem, vmem],
        out_shape=[
            jax.ShapeDtypeStruct((1, own_rows), jnp.float32),
            jax.ShapeDtypeStruct((1, ids.shape[0]), jnp.float32),
        ],
        scratch_shapes=[pltpu.VMEM((128, 128), jnp.float32)],
        compiler_params=pltpu.CompilerParams(vmem_limit_bytes=32 * 2**20),
        name="finish",
    )(own.reshape(1), row, offset, back, lse_prev)
    return lse_now.reshape(-1), rerank


def solution(mesh):
    across, ways = mesh.devices.shape
    split = Mesh(mesh.devices.reshape(across // 8, 4, 2, ways), ALL)
    shard = ("z", "y", "core")
    return jax.shard_map(
        local,
        mesh=split,
        in_specs=(P(ALL, None), P(shard, None), P(ALL, None), P(ALL, None), P(ALL, None), P(ALL)),
        out_specs=(P(ALL), P(ALL, None)),
        check_vma=False,
    )
```

time: 640 us -> 116 us (0.18)
  waiting for transfers between devices: 373 us -> 31.7 us
  local copies, waits for them, and re-layouts: 167 us -> 4.7 us
  matrix products: 20.9 us -> 0 us
  between operations: 14.6 us -> 1.42 us
  starting transfers between devices: 13.5 us -> 24.3 us
  blocking collectives: 36 us -> 46.1 us
    all_gather x3 -> x0, waiting for transfers between devices: 286 us -> none  [the longest x2 145 us: merged(): gathered = jax.tree.map(lambda a: lax.all_gather(a, axis), part)]
    dynamic_slice x131 -> x0, local copies, waits for them, and re-layouts: 137 us -> none  [take(): lax.dynamic_index_in_dim(a, source, 0, False)]
    all_to_all x2, waiting for transfers between devices: 86.1 us -> 31.7 us  [the longest x1 18.1 us: local(): back = lax.all_to_all(merged, BACK, 0, 0, tiled=True)]
    all_gather x1 -> x2, blocking collectives: 10.5 us -> 35.9 us  [the longest x1 33.5 us: local(): column = lax.all_gather(sent, 'z')]
    dot_general x19 -> x0, matrix products: 20.9 us -> none  [the longest x16 19.6 us: score_block(): lax.dot_general(block_rows, prefix_rows, (((1,), (1,)), ((), ())), prefer...]
    all_to_all x1, blocking collectives: 25.5 us -> 10.2 us  [local(): lax.all_to_all(jnp.broadcast_to(asked[None], (lax.axis_size('y'),) + aske...]
    unnamed x10 -> x11, local copies, waits for them, and re-layouts: 16.2 us -> 2 us
    all_to_all x2, starting transfers between devices: 13.4 us -> 24.3 us  [the longest x1 14.1 us: local(): lax.all_to_all(jnp.broadcast_to(prefixes[None], (plane * lax.axis_size('x...]
  transfers between devices with their start and end apart: 5 -> 2, of which waited for: 5 -> 2; matrix products, arithmetic and copies ran while one was open for 3% -> 0% of each run, Pallas kernels for 0% -> 0%
where the time goes in v1:
time: 116 us
  blocking collectives  46.1 us (40%)
  waiting for transfers between devices  31.7 us (27%)
  starting transfers between devices  24.3 us (21%)
  Pallas kernels  5.16 us (4%)
  local copies, waits for them, and re-layouts  4.7 us (4%)
  other arithmetic  2.29 us (2%)
  between operations  1.42 us (1%)
    all_gather x1, blocking collectives, local(): column = lax.all_gather(sent, 'z')  33.5 us
    all_to_all x1, waiting for transfers between devices, local(): back = lax.all_to_all(merged, BACK, 0, 0, tiled=True)  18.1 us
    all_to_all x1, starting transfers between devices, local(): lax.all_to_all(jnp.broadcast_to(prefixes[None], (plane * lax.axis_size('x...  14.1 us
    all_to_all x1, waiting for transfers between devices, local(): lax.all_to_all(jnp.broadcast_to(prefixes[None], (plane * lax.axis_size('x...  13.6 us
    all_to_all x1, blocking collectives, local(): lax.all_to_all(jnp.broadcast_to(asked[None], (lax.axis_size('y'),) + aske...  10.2 us
    all_to_all x1, starting transfers between devices, local(): back = lax.all_to_all(merged, BACK, 0, 0, tiled=True)  10.2 us
    pallas_call x1, Pallas kernels, local(): pl.pallas_call(lambda *refs: partial_lse(head ** (-0.5), *refs), grid=(de...  3.17 us
    all_gather x1, blocking collectives, local(): asked = lax.all_gather(asked, 'core', tiled=True)  2.37 us
  transfers between devices with their start and end apart: 2, of which 2 were waited for; matrix products, arithmetic and copies ran while one was open for 0% of the time, Pallas kernels for 0%

profile of v1, /device:TPU:1, one launch (start us, length us, event | category | flops | bytes accessed | tf_op | source)
XLA Modules:
  0.0 115.7 jit_solution(6588295520798384280)
XLA Ops:
  0.6 0.0 copy-start.3
  0.6 0.8 reduce
  1.4 0.1 pad.4.clone
  1.5 0.8 maximum_maximum_fusion
  2.3 33.5 %all-gather = bf16[1280,256]{1,0:T(8,128)(2,1)S(1)} all-gather(bf16[80,256]{1,0:T(8,128)(2,1)S(1)} %maximum_maximum_fusion), channel_id=2, replica_groups=mesh['z'=16,'y'=4,'core'=2,'x'=4] {'z'}, dimensions={0}, use_global_device_ids=true | all-gather | bytes 696320 | tf_op jit(solution)/shard_map/all_gather | solution.py:81
  35.9 0.0 copy-start.1
  35.9 0.9 copy-done.1
  36.8 10.2 %all_to_all.21 = bf16[4,16,3072]{2,1,0:T(8,128)(2,1)S(1)} all-to-all(bf16[4,16,3072]{2,1,0:T(8,128)(2,1)S(1)} %broadcast_in_dim.18), channel_id=1, replica_groups=mesh['z'=16,'y'=4,'core'=2,'x'=4] {'y'}, dimensions={0} | all-to-all | bytes 786432 | tf_op jit(solution)/shard_map/all_to_all | solution.py:84
  47.0 0.0 copy-done.3
  47.0 1.1 broadcast_in_dim.19
  48.1 14.1 %all-to-all-start.1 = ((bf16[32,64,256]{2,1,0:T(8,128)(2,1)}), bf16[32,64,256]{2,1,0:T(8,128)(2,1)S(1)}, u32[]{:S(2)}, u32[]{:S(2)}) async-start(bf16[32,64,256]{2,1,0:T(8,128)(2,1)} %broadcast_in_dim.19), calls=%async_computation.1 | async-start | bytes 2097152 | tf_op jit(solution)/shard_map/all_to_all | solution.py:74
  62.2 2.4 %all_gather.11.asked_ref = bf16[128,3072]{1,0:T(8,128)(2,1)S(1)} all-gather(bf16[64,3072]{1,0:T(8,128)(2,1)S(1)} %bitcast.37), channel_id=1, replica_groups=mesh['z'=16,'y'=4,'core'=2,'x'=4] {'core'}, dimensions={0}, use_global_device_ids=true | all-gather | bytes 1179648 | tf_op jit(solution)/shard_map/all_gather | solution.py:87
  64.6 13.6 %all-to-all-done.1 = bf16[32,64,256]{2,1,0:T(8,128)(2,1)S(1)} async-done(((bf16[32,64,256]{2,1,0:T(8,128)(2,1)}), bf16[32,64,256]{2,1,0:T(8,128)(2,1)S(1)}, u32[]{:S(2)}, u32[]{:S(2)}) %all-to-all-start.1) | async-done | bytes 1048608 | tf_op jit(solution)/shard_map/all_to_all | solution.py:74
  78.2 1.1 copy-done.2
  79.3 3.2 %partial_lse.1 = f32[1,1024]{1,0:T(1,128)S(1)} custom-call(bf16[16,80,256]{2,1,0:T(8,128)(2,1)S(1)} %bitcast.35, bf16[2048,256]{1,0:T(8,128)(2,1)S(1)} %bitcast.32), custom_call_target="tpu_custom_call" | custom-call | flops 536870912 | bytes 2097152 | tf_op jit(solution)/shard_map/partial_lse/pallas_call | solution.py:90
  82.5 0.5 broadcast.49
  83.0 0.7 reduce.4
  83.7 0.1 tile.10
  83.7 0.0 copy-done
  83.8 0.6 passage_scores.1
  84.4 0.9 copy.9
  85.3 10.2 %all-to-all-start.2 = ((f32[128,1,320]{2,1,0:T(1,128)}), f32[128,1,320]{2,1,0:T(1,128)S(1)}, u32[]{:S(2)}, u32[]{:S(2)}) async-start(f32[128,1,320]{2,1,0:T(1,128)} %copy.9), calls=%async_computation.2 | async-start | bytes 393216 | tf_op jit(solution)/shard_map/all_to_all | solution.py:119
  96.2 18.1 %all-to-all-done.2 = f32[128,1,320]{2,1,0:T(1,128)S(1)} async-done(((f32[128,1,320]{2,1,0:T(1,128)}), f32[128,1,320]{2,1,0:T(1,128)S(1)}, u32[]{:S(2)}, u32[]{:S(2)}) %all-to-all-start.2) | async-done | bytes 163872 | tf_op jit(solution)/shard_map/all_to_all | solution.py:119
  114.4 1.4 %finish.1 = (f32[1,64]{1,0:T(1,128)}, f32[1,100]{1,0:T(1,128)}) custom-call(s32[1]{0:T(128)} %bitcast.refs_0_, s32[100]{0:T(128)S(1)} %get-tuple-element.7.refs_1_, s32[100]{0:T(128)S(1)} %get-tuple-element.6.refs_2_, f32[128,320]{1,0:T(8,128)S(1)} %bitcast.36, f32[1]{0:T(128)S(6)} %copy.16.refs_4_), custom_call_target="tpu_custom_call" | custom-call | tf_op jit(solution)/shard_map/finish/pallas_call | solution.py:126
  (13 shorter events, 0.2 us)
Async XLA Ops:
  0.6 46.4 %copy-start.3 = (bf16[64,256]{1,0:T(8,128)(2,1)S(1)}, bf16[64,256]{1,0:T(8,128)(2,1)}, u32[]{:S(2)}) copy-start(bf16[64,256]{1,0:T(8,128)(2,1)} %param.6) | copy-start | bytes 98308
  35.9 0.9 copy-start.1
  48.1 30.1 %all-to-all-start.1 = ((bf16[32,64,256]{2,1,0:T(8,128)(2,1)}), bf16[32,64,256]{2,1,0:T(8,128)(2,1)S(1)}, u32[]{:S(2)}, u32[]{:S(2)}) async-start(bf16[32,64,256]{2,1,0:T(8,128)(2,1)} %broadcast_in_dim.19), calls=%async_computation.1 | async-start | bytes 2097152 | tf_op jit(solution)/shard_map/all_to_all | solution.py:74
  78.2 1.1 copy-start.2
  79.3 4.4 %copy-start = (bf16[256,2816]{1,0:T(8,128)(2,1)S(1)}, bf16[256,2816]{1,0:T(8,128)(2,1)}, u32[]{:S(2)}) copy-start(bf16[256,2816]{1,0:T(8,128)(2,1)} %tails_ref.1) | copy-start | bytes 4325380
  83.8 12.4 %copy-start.4 = (s32[1,100]{1,0:T(1,128)S(1)}, s32[1,100]{1,0:T(1,128)}, u32[]{:S(2)}) copy-start(s32[1,100]{1,0:T(1,128)} %param.10) | copy-start | bytes 1204
  85.3 29.0 %all-to-all-start.2 = ((f32[128,1,320]{2,1,0:T(1,128)}), f32[128,1,320]{2,1,0:T(1,128)S(1)}, u32[]{:S(2)}, u32[]{:S(2)}) async-start(f32[128,1,320]{2,1,0:T(1,128)} %copy.9), calls=%async_computation.2 | async-start | bytes 393216 | tf_op jit(solution)/shard_map/all_to_all | solution.py:119

commit v2 on v1

v2 whole, which is shorter than its diff:
```python
import jax
import jax.numpy as jnp
from jax import lax
from jax.experimental import pallas as pl
from jax.experimental.pallas import tpu as pltpu
from jax.sharding import Mesh, PartitionSpec as P

ALL = ("z", "y", "core", "x")
PLANE = ("y", "core", "x")
BACK = ("core", "y", "z")
LOG2E = 1.4426950408889634
LANES = 128


def partial_lse(scale, rows, queries_ref, passages_ref, out_ref, scores):
    groups = queries_ref.shape[0]
    width = passages_ref.shape[1]
    block = queries_ref[:, :rows, :].reshape(groups * rows, width)
    count, step = passages_ref.shape[0], 256
    top = None
    for start in range(0, count, step):
        part = lax.dot_general(
            passages_ref[start : start + step, :],
            block,
            (((1,), (1,)), ((), ())),
            preferred_element_type=jnp.float32,
        )
        scores[start : start + step, :] = part
        high = jnp.max(part.reshape(step // 8, 8, groups * rows), axis=0)
        top = high if top is None else jnp.maximum(top, high)
    peak = jnp.max(top, axis=0, keepdims=True)
    total = None
    for start in range(0, count, step):
        part = jnp.exp2((scores[start : start + step, :] - peak) * (scale * LOG2E))
        added = jnp.sum(part.reshape(step // 8, 8, groups * rows), axis=0)
        total = added if total is None else total + added
    found = peak * scale + jnp.log(jnp.sum(total, axis=0, keepdims=True))
    first = pl.program_id(0) * groups

    @pl.when(first == 0)
    def _():
        out_ref[...] = jnp.zeros_like(out_ref)

    for group in range(groups):
        out_ref[pl.ds(first + group, 1), :rows] = found[:, group * rows : (group + 1) * rows]


def listed_scores(rows, place_ref, asked_ref, prefixes_ref, tails_ref, parts_ref, out_ref):
    shard_rows, head = tails_ref.shape[0], prefixes_ref.shape[1]
    full = head + tails_ref.shape[1]
    start = pl.multiple_of(place_ref[0] * shard_rows, shard_rows)
    dims = (((1,), (1,)), ((), ()))
    scores = lax.dot_general(
        asked_ref[:, :head], prefixes_ref[pl.ds(start, shard_rows), :], dims, preferred_element_type=jnp.float32
    ) + lax.dot_general(asked_ref[:, head:full], tails_ref[...], dims, preferred_element_type=jnp.float32)
    count = asked_ref.shape[0]
    shards = asked_ref[:, full : full + LANES].astype(jnp.float32)
    offsets = asked_ref[:, full + LANES : full + 2 * LANES].astype(jnp.float32)
    lanes = lax.broadcasted_iota(jnp.int32, (count, LANES), 1)
    mine = shards == place_ref[1].astype(jnp.float32)
    key = lanes.astype(jnp.float32) * shard_rows + offsets
    low = jnp.min(jnp.where(mine, key, float(LANES * shard_rows)), axis=1, keepdims=True)
    high = jnp.max(jnp.where(mine, key, 0.0), axis=1, keepdims=True)
    column = lax.broadcasted_iota(jnp.int32, scores.shape, 1)

    def pick(at):
        at = (at - jnp.floor(at * (1.0 / shard_rows)) * shard_rows).astype(jnp.int32)
        return jnp.sum(jnp.where(column == at, scores, 0.0), axis=1, keepdims=True)

    depth = parts_ref.shape[0]
    parts = jnp.concatenate([parts_ref[...]] * (count // depth), axis=0)
    out_ref[...] = jnp.where(lanes < rows, parts, jnp.where(lanes == rows, pick(low), pick(high)))


def finish(scale, rows, depth, own_ref, row_ref, second_ref, back_ref, prev_ref, lse_ref, rerank_ref):
    count = rerank_ref.shape[1]
    start = pl.multiple_of(own_ref[0] * depth, depth)
    parts = back_ref[pl.ds(start, depth), :rows]
    peak = jnp.max(parts, axis=0, keepdims=True)
    lse_ref[...] = peak + jnp.log(jnp.sum(jnp.exp(parts - peak), axis=0, keepdims=True))
    turned = back_ref[...].T
    shape = (8, LANES)
    at = jnp.broadcast_to(row_ref[...], shape)
    low = jnp.take_along_axis(jnp.broadcast_to(turned[rows : rows + 1, :], shape), at, axis=1)
    high = jnp.take_along_axis(jnp.broadcast_to(turned[rows + 1 : rows + 2, :], shape), at, axis=1)
    values = jnp.where(second_ref[...] > 0, high[:1], low[:1])
    rerank_ref[...] = values[:, :count] * scale - prev_ref[0]


def local(prefixes, tails, queries_now, queries_prev, candidates, lse_prev):
    vmem, smem = pl.BlockSpec(memory_space=pltpu.VMEM), pl.BlockSpec(memory_space=pltpu.SMEM)
    depth, ys, cores = lax.axis_size("z"), lax.axis_size("y"), lax.axis_size("core")
    own_rows, head = queries_now.shape
    shard_rows = tails.shape[0]
    full_width = queries_prev.shape[1]
    plane = ys * cores
    turn = depth // 2
    around = [(i + turn) % depth for i in range(depth)]

    ids = candidates.reshape(-1)
    count = ids.shape[0]
    shard, offset = ids // shard_rows, ids % shard_rows
    listed = jnp.concatenate(
        [jnp.pad(shard, (0, LANES - count), constant_values=-1), jnp.pad(offset, (0, LANES - count))]
    ).astype(queries_prev.dtype)

    passages = lax.all_to_all(
        jnp.broadcast_to(prefixes[None], (plane * lax.axis_size("x"),) + prefixes.shape),
        PLANE, 0, 0, tiled=True,
    ).reshape(-1, head)

    extra = full_width // head + 1
    sent = jnp.concatenate(
        [
            queries_now,
            queries_prev.reshape(extra - 1, head),
            listed.reshape(1, head),
            jnp.zeros((-extra % 16, head), queries_now.dtype),
        ]
    )
    column = lax.all_gather(sent, "z", axis_index_groups=[around])
    asked = column[:, own_rows : own_rows + extra].reshape(depth, extra * head)

    asked = jnp.broadcast_to(asked[None], (ys,) + asked.shape)
    asked, passages = lax.optimization_barrier((asked, passages))
    asked = lax.all_to_all(asked, "y", 0, 0, tiled=True).reshape(-1, extra * head)
    asked = lax.all_gather(asked, "core", tiled=True)

    step = 4
    parts = pl.pallas_call(
        lambda *refs: partial_lse(head**-0.5, own_rows, *refs),
        grid=(depth // step,),
        in_specs=[
            pl.BlockSpec((step,) + column.shape[1:], lambda i: (i, 0, 0)),
            pl.BlockSpec(passages.shape, lambda i: (0, 0)),
        ],
        out_specs=pl.BlockSpec((depth, LANES), lambda i: (0, 0)),
        out_shape=jax.ShapeDtypeStruct((depth, LANES), jnp.float32),
        scratch_shapes=[pltpu.VMEM((passages.shape[0], step * own_rows), jnp.float32)],
        compiler_params=pltpu.CompilerParams(vmem_limit_bytes=32 * 2**20),
        cost_estimate=pl.CostEstimate(flops=2 * 2**28, bytes_accessed=2 * 2**20, transcendentals=2**21),
        name="partial_lse",
    )(column, passages)

    z, y, core = lax.axis_index("z"), lax.axis_index("y"), lax.axis_index("core")
    place = y * cores + core
    merged = pl.pallas_call(
        lambda *refs: listed_scores(own_rows, *refs),
        in_specs=[smem, vmem, vmem, vmem, vmem],
        out_specs=vmem,
        out_shape=jax.ShapeDtypeStruct((plane * depth, LANES), jnp.float32),
        compiler_params=pltpu.CompilerParams(vmem_limit_bytes=32 * 2**20),
        cost_estimate=pl.CostEstimate(flops=2 * 128 * 256 * 3072, bytes_accessed=3 * 2**20, transcendentals=0),
        name="listed_scores",
    )(jnp.stack([place, z * plane + place]), asked, passages, tails, parts)

    groups = [base + i for base in range(0, plane * depth, depth) for i in around]
    back = lax.all_to_all(merged, BACK, 0, 0, tiled=True, axis_index_groups=[groups])

    row = (shard % cores) * (ys * depth) + (shard // cores % ys) * depth + (shard // plane + turn) % depth
    before = jnp.arange(count)[:, None] > jnp.arange(count)[None, :]
    second = jnp.any((shard[:, None] == shard[None, :]) & before, axis=1).astype(jnp.int32)
    lse_now, rerank = pl.pallas_call(
        lambda *refs: finish(full_width**-0.5, own_rows, depth, *refs),
        in_specs=[smem, vmem, vmem, vmem, smem],
        out_specs=[vmem, vmem],
        out_shape=[
            jax.ShapeDtypeStruct((1, own_rows), jnp.float32),
            jax.ShapeDtypeStruct((1, count), jnp.float32),
        ],
        compiler_params=pltpu.CompilerParams(vmem_limit_bytes=32 * 2**20),
        name="finish",
    )(
        (core * ys + y).reshape(1),
        jnp.pad(row, (0, LANES - count)).reshape(1, LANES),
        jnp.pad(second, (0, LANES - count)).reshape(1, LANES),
        back,
        lse_prev,
    )
    return lse_now.reshape(-1), rerank


def solution(mesh):
    across, ways = mesh.devices.shape
    split = Mesh(mesh.devices.reshape(across // 8, 4, 2, ways), ALL)
    shard = ("z", "y", "core")
    return jax.shard_map(
        local,
        mesh=split,
        in_specs=(P(ALL, None), P(shard, None), P(ALL, None), P(ALL, None), P(ALL, None), P(ALL)),
        out_specs=(P(ALL), P(ALL, None)),
        check_vma=False,
    )
```

time: 116 us -> 89.4 us (0.77)
  waiting for transfers between devices: 31.7 us -> 8.06 us
  blocking collectives: 46.1 us -> 41.3 us
  starting transfers between devices: 24.3 us -> 28.9 us
  local copies, waits for them, and re-layouts: 4.7 us -> 2.82 us
  other arithmetic: 2.29 us -> 0.42 us
    all_to_all x1, waiting for transfers between devices: 13.6 us -> 0.01 us  [local(): lax.all_to_all(jnp.broadcast_to(prefixes[None], (plane * lax.axis_size('x...]
    all_to_all x1 -> x0, blocking collectives: 10.2 us -> none  [local(): lax.all_to_all(jnp.broadcast_to(asked[None], (lax.axis_size('y'),) + aske...]
    all_to_all x1 -> x2, waiting for transfers between devices: 18.1 us -> 8.05 us  [the longest x1 5.1 us: local(): lax.all_to_all(merged, BACK, 0, 0, tiled=True, axis_index_groups=[groups])]
    all_to_all x1 -> x2, starting transfers between devices: 10.2 us -> 18.5 us  [the longest x1 14.3 us: local(): lax.all_to_all(merged, BACK, 0, 0, tiled=True, axis_index_groups=[groups])]
    all_gather x1, blocking collectives: 2.37 us -> 10.2 us  [local(): asked = lax.all_gather(asked, 'core', tiled=True)]
    all_to_all x1, starting transfers between devices: 14.1 us -> 10.5 us  [local(): lax.all_to_all(jnp.broadcast_to(prefixes[None], (plane * lax.axis_size('x...]
    all_gather x1, blocking collectives: 33.5 us -> 31.2 us  [local(): column = lax.all_gather(sent, 'z', axis_index_groups=[around])]
    unnamed x11 -> x9, local copies, waits for them, and re-layouts: 2 us -> 0.06 us
  transfers between devices with their start and end apart: 2 -> 3, of which waited for: 2 -> 2; matrix products, arithmetic and copies ran while one was open for 0% -> 1% of each run, Pallas kernels for 0% -> 4%
where the time goes in v2:
time: 89.4 us; the launch traced here: 89 us
  blocking collectives  41.3 us (46%)
  starting transfers between devices  28.9 us (32%)
  waiting for transfers between devices  8.06 us (9%)
  Pallas kernels  5.99 us (7%)
  local copies, waits for them, and re-layouts  2.82 us (3%)
  between operations  1.45 us (2%)
    all_gather x1, blocking collectives, local(): column = lax.all_gather(sent, 'z', axis_index_groups=[around])  31.2 us
    all_to_all x1, starting transfers between devices, local(): lax.all_to_all(merged, BACK, 0, 0, tiled=True, axis_index_groups=[groups])  14.3 us
    all_to_all x1, starting transfers between devices, local(): lax.all_to_all(jnp.broadcast_to(prefixes[None], (plane * lax.axis_size('x...  10.5 us
    all_gather x1, blocking collectives, local(): asked = lax.all_gather(asked, 'core', tiled=True)  10.2 us
    all_to_all x1, waiting for transfers between devices, local(): lax.all_to_all(merged, BACK, 0, 0, tiled=True, axis_index_groups=[groups])  5.1 us
    all_to_all x1, starting transfers between devices, local(): lax.all_to_all(asked, 'y', 0, 0, tiled=True).reshape(-1, extra * head)  4.16 us
    pallas_call x1, Pallas kernels, local(): pl.pallas_call(lambda *refs: partial_lse(head ** (-0.5), own_rows, *refs)...  3.45 us
    all_to_all x1, waiting for transfers between devices, local(): lax.all_to_all(asked, 'y', 0, 0, tiled=True).reshape(-1, extra * head)  2.96 us
  transfers between devices with their start and end apart: 3, of which 2 were waited for; matrix products, arithmetic and copies ran while one was open for 1% of the time, Pallas kernels for 4%

profile of v2, /device:TPU:1, one launch (start us, length us, event | category | flops | bytes accessed | tf_op | source)
XLA Modules:
  0.0 89.0 jit_solution(10604435529061260284)
XLA Ops:
  0.6 0.0 copy-start.2
  0.6 0.0 copy-start.3
  0.7 0.0 copy-start.1
  0.7 1.9 %broadcast_in_dim.11 = bf16[32,64,256]{2,1,0:T(8,128)(2,1)} broadcast(bf16[64,256]{1,0:T(8,128)(2,1)} %param.6), dimensions={1,2} | broadcast | bytes 1081344 | tf_op jit(solution)/shard_map/broadcast_in_dim | solution.py:108
  2.5 10.5 %all-to-all-start = ((bf16[32,64,256]{2,1,0:T(8,128)(2,1)}), bf16[32,64,256]{2,1,0:T(8,128)(2,1)S(1)}, u32[]{:S(2)}, u32[]{:S(2)}) async-start(bf16[32,64,256]{2,1,0:T(8,128)(2,1)} %broadcast_in_dim.11), calls=%async_computation | async-start | bytes 2097152 | tf_op jit(solution)/shard_map/all_to_all | solution.py:107
  13.0 0.0 copy-done.2
  13.1 0.1 pad.24.clone
  13.2 0.0 copy-done.3
  13.2 0.0 copy-done.1
  13.2 0.1 maximum_maximum_fusion
  13.3 31.2 %all-gather = bf16[1280,256]{1,0:T(8,128)(2,1)S(1)} all-gather(bf16[80,256]{1,0:T(8,128)(2,1)S(1)} %maximum_maximum_fusion), channel_id=2, replica_groups={{256,288,320,352,384,416,448,480,0,32,64,96,128,160,192,224},{257,289,3..., dimensions={0}, use_global_device_ids=true | all-gather | bytes 696320 | tf_op jit(solution)/shard_map/all_gather | solution.py:121
  44.6 0.0 all-to-all-done
  44.6 0.8 broadcast_in_dim.10
  45.4 4.2 %all-to-all-start.1 = ((bf16[4,16,3328]{2,1,0:T(8,128)(2,1)}), bf16[4,16,3328]{2,1,0:T(8,128)(2,1)}, u32[]{:S(2)}, u32[]{:S(2)}) async-start(bf16[4,16,3328]{2,1,0:T(8,128)(2,1)} %broadcast_in_dim.10), calls=%async_computation.1 | async-start | bytes 851968 | tf_op jit(solution)/shard_map/all_to_all | solution.py:126
  49.5 0.1 pad_add_fusion.refs_0_
  49.6 0.0 copy-start
  49.6 3.4 %partial_lse.1.refs_4_ = f32[16,128]{1,0:T(8,128)S(1)} custom-call(bf16[16,80,256]{2,1,0:T(8,128)(2,1)S(1)} %bitcast.42, bf16[2048,256]{1,0:T(8,128)(2,1)S(1)} %bitcast.39), custom_call_target="tpu_custom_call" | custom-call | flops 536870912 | bytes 2097152 | tf_op jit(solution)/shard_map/partial_lse/pallas_call | solution.py:130
  53.1 3.0 %all-to-all-done.1 = bf16[4,16,3328]{2,1,0:T(8,128)(2,1)} async-done(((bf16[4,16,3328]{2,1,0:T(8,128)(2,1)}), bf16[4,16,3328]{2,1,0:T(8,128)(2,1)}, u32[]{:S(2)}, u32[]{:S(2)}) %all-to-all-start.1) | async-done | bytes 426016 | tf_op jit(solution)/shard_map/all_to_all | solution.py:126
  56.0 10.2 %all_gather.11.refs_1_ = bf16[128,3328]{1,0:T(8,128)(2,1)S(1)} all-gather(bf16[64,3328]{1,0:T(8,128)(2,1)} %bitcast.11), channel_id=1, replica_groups=mesh['z'=16,'y'=4,'core'=2,'x'=4] {'core'}, dimensions={0}, use_global_device_ids=true | all-gather | bytes 1277952 | tf_op jit(solution)/shard_map/all_gather | solution.py:127
  66.2 1.9 %listed_scores.1 = f32[128,128]{1,0:T(8,128)} custom-call(s32[2]{0:T(128)S(1)} %pad_add_fusion.refs_0_, bf16[128,3328]{1,0:T(8,128)(2,1)S(1)} %all_gather.11.refs_1_, bf16[2048,256]{1,0:T(8,128)(2,1)S(1)} %bitcast.40, bf16[256,2816]{1,0:T(8,128)(2,1)S(1)} %copy-done, f32[16,128]{1,0:T(8,128)S(1)} %partial_lse.1.refs_4_), custom_call_target="tpu_custom_call" | custom-call | flops 201326592 | bytes 3145728 | tf_op jit(solution)/shard_map/listed_scores/pallas_call | solution.py:147
  68.1 14.3 %all-to-all-start.2 = ((f32[128,1,128]{2,1,0:T(1,128)}), f32[128,1,128]{2,1,0:T(1,128)S(1)}, u32[]{:S(2)}, u32[]{:S(2)}) async-start(f32[128,1,128]{2,1,0:T(1,128)} %bitcast.13), calls=%async_computation.2 | async-start | bytes 131072 | tf_op jit(solution)/shard_map/all_to_all | solution.py:158
  82.4 0.2 fusion.1
  83.3 5.1 %all-to-all-done.2 = f32[128,1,128]{2,1,0:T(1,128)S(1)} async-done(((f32[128,1,128]{2,1,0:T(1,128)}), f32[128,1,128]{2,1,0:T(1,128)S(1)}, u32[]{:S(2)}, u32[]{:S(2)}) %all-to-all-start.2) | async-done | bytes 65568 | tf_op jit(solution)/shard_map/all_to_all | solution.py:158
  88.4 0.7 finish.1
  (12 shorter events, 0.2 us)
Async XLA Ops:
  0.6 12.4 %copy-start.2 = (bf16[1,3072]{1,0:T(2,128)(2,1)S(1)}, bf16[1,3072]{1,0:T(2,128)(2,1)}, u32[]{:S(2)}) copy-start(bf16[1,3072]{1,0:T(2,128)(2,1)} %param.9) | copy-start | bytes 18436
  0.6 12.5 %copy-start.3 = (s32[1,100]{1,0:T(1,128)S(1)}, s32[1,100]{1,0:T(1,128)}, u32[]{:S(2)}) copy-start(s32[1,100]{1,0:T(1,128)} %param.10) | copy-start | bytes 1204
  0.7 12.6 %copy-start.1 = (bf16[64,256]{1,0:T(8,128)(2,1)S(1)}, bf16[64,256]{1,0:T(8,128)(2,1)}, u32[]{:S(2)}) copy-start(bf16[64,256]{1,0:T(8,128)(2,1)} %param.8) | copy-start | bytes 98308
  2.5 42.0 %all-to-all-start = ((bf16[32,64,256]{2,1,0:T(8,128)(2,1)}), bf16[32,64,256]{2,1,0:T(8,128)(2,1)S(1)}, u32[]{:S(2)}, u32[]{:S(2)}) async-start(bf16[32,64,256]{2,1,0:T(8,128)(2,1)} %broadcast_in_dim.11), calls=%async_computation | async-start | bytes 2097152 | tf_op jit(solution)/shard_map/all_to_all | solution.py:107
  45.4 10.7 %all-to-all-start.1 = ((bf16[4,16,3328]{2,1,0:T(8,128)(2,1)}), bf16[4,16,3328]{2,1,0:T(8,128)(2,1)}, u32[]{:S(2)}, u32[]{:S(2)}) async-start(bf16[4,16,3328]{2,1,0:T(8,128)(2,1)} %broadcast_in_dim.10), calls=%async_computation.1 | async-start | bytes 851968 | tf_op jit(solution)/shard_map/all_to_all | solution.py:126
  49.6 16.6 %copy-start = (bf16[256,2816]{1,0:T(8,128)(2,1)S(1)}, bf16[256,2816]{1,0:T(8,128)(2,1)}, u32[]{:S(2)}) copy-start(bf16[256,2816]{1,0:T(8,128)(2,1)} %refs_3_.1) | copy-start | bytes 4325380
  68.1 20.3 %all-to-all-start.2 = ((f32[128,1,128]{2,1,0:T(1,128)}), f32[128,1,128]{2,1,0:T(1,128)S(1)}, u32[]{:S(2)}, u32[]{:S(2)}) async-start(f32[128,1,128]{2,1,0:T(1,128)} %bitcast.13), calls=%async_computation.2 | async-start | bytes 131072 | tf_op jit(solution)/shard_map/all_to_all | solution.py:158

commit v3 on v2

--- a/solution.py
+++ b/solution.py
@@ -6,8 +6,9 @@
 from jax.sharding import Mesh, PartitionSpec as P
 
 ALL = ("z", "y", "core", "x")
-PLANE = ("y", "core", "x")
-BACK = ("core", "y", "z")
+PLANE = ("core", "y", "x")
+BACK = ("z", "y", "core")
+PAIR = ("z", "core")
 LOG2E = 1.4426950408889634
 LANES = 128
 
@@ -118,13 +119,15 @@
             jnp.zeros((-extra % 16, head), queries_now.dtype),
         ]
     )
-    column = lax.all_gather(sent, "z", axis_index_groups=[around])
+    rings = [[z * cores + (z + ring) % cores for z in around] for ring in range(cores)]
+    column = lax.all_gather(sent, PAIR, axis_index_groups=rings)
     asked = column[:, own_rows : own_rows + extra].reshape(depth, extra * head)
 
     asked = jnp.broadcast_to(asked[None], (ys,) + asked.shape)
     asked, passages = lax.optimization_barrier((asked, passages))
     asked = lax.all_to_all(asked, "y", 0, 0, tiled=True).reshape(-1, extra * head)
-    asked = lax.all_gather(asked, "core", tiled=True)
+    pairs = [[z * cores + (z + ring) % cores for ring in range(cores)] for z in range(depth)]
+    asked = lax.all_gather(asked, PAIR, tiled=True, axis_index_groups=pairs)
 
     step = 4
     parts = pl.pallas_call(
@@ -152,12 +155,13 @@
         compiler_params=pltpu.CompilerParams(vmem_limit_bytes=32 * 2**20),
         cost_estimate=pl.CostEstimate(flops=2 * 128 * 256 * 3072, bytes_accessed=3 * 2**20, transcendentals=0),
         name="listed_scores",
-    )(jnp.stack([place, z * plane + place]), asked, passages, tails, parts)
+    )(jnp.stack([core * ys + y, z * plane + place]), asked, passages, tails, parts)
 
-    groups = [base + i for base in range(0, plane * depth, depth) for i in around]
+    groups = [z * plane + i * cores + (z + ring) % cores for ring in range(cores) for i in range(ys) for z in around]
     back = lax.all_to_all(merged, BACK, 0, 0, tiled=True, axis_index_groups=[groups])
 
-    row = (shard % cores) * (ys * depth) + (shard // cores % ys) * depth + (shard // plane + turn) % depth
+    far = shard // plane
+    row = ((shard + far) % cores * ys + shard // cores % ys) * depth + (far + turn) % depth
     before = jnp.arange(count)[:, None] > jnp.arange(count)[None, :]
     second = jnp.any((shard[:, None] == shard[None, :]) & before, axis=1).astype(jnp.int32)
     lse_now, rerank = pl.pallas_call(
@@ -171,7 +175,7 @@
         compiler_params=pltpu.CompilerParams(vmem_limit_bytes=32 * 2**20),
         name="finish",
     )(
-        (core * ys + y).reshape(1),
+        ((core + z) % cores * ys + y).reshape(1),
         jnp.pad(row, (0, LANES - count)).reshape(1, LANES),
         jnp.pad(second, (0, LANES - count)).reshape(1, LANES),
         back,

time: 89.4 us -> 87.6 us (0.980)
  blocking collectives: 41.3 us -> 38.8 us
    all_gather x2, blocking collectives: 41.3 us -> 38.8 us  [the longest x1 34.7 us: local(): column = lax.all_gather(sent, PAIR, axis_index_groups=rings)]
    all_to_all x1, waiting for transfers between devices: 2.96 us -> 4.09 us  [local(): lax.all_to_all(asked, 'y', 0, 0, tiled=True).reshape(-1, extra * head)]
where the time goes in v3:
time: 87.6 us; the launch traced here: 87.2 us
  blocking collectives  38.8 us (44%)
  starting transfers between devices  29 us (33%)
  waiting for transfers between devices  8.75 us (10%)
  Pallas kernels  5.99 us (7%)
  local copies, waits for them, and re-layouts  2.82 us (3%)
  between operations  1.45 us (2%)
    all_gather x1, blocking collectives, local(): column = lax.all_gather(sent, PAIR, axis_index_groups=rings)  34.7 us
    all_to_all x1, starting transfers between devices, local(): lax.all_to_all(merged, BACK, 0, 0, tiled=True, axis_index_groups=[groups])  14.3 us
    all_to_all x1, starting transfers between devices, local(): lax.all_to_all(jnp.broadcast_to(prefixes[None], (plane * lax.axis_size('x...  10.6 us
    all_to_all x1, waiting for transfers between devices, local(): lax.all_to_all(merged, BACK, 0, 0, tiled=True, axis_index_groups=[groups])  4.65 us
    all_to_all x1, starting transfers between devices, local(): lax.all_to_all(asked, 'y', 0, 0, tiled=True).reshape(-1, extra * head)  4.13 us
    all_to_all x1, waiting for transfers between devices, local(): lax.all_to_all(asked, 'y', 0, 0, tiled=True).reshape(-1, extra * head)  4.09 us
    all_gather x1, blocking collectives, local(): asked = lax.all_gather(asked, PAIR, tiled=True, axis_index_groups=pairs)  4.08 us
    pallas_call x1, Pallas kernels, local(): pl.pallas_call(lambda *refs: partial_lse(head ** (-0.5), own_rows, *refs)...  3.45 us
  transfers between devices with their start and end apart: 3, of which 2 were waited for; matrix products, arithmetic and copies ran while one was open for 1% of the time, Pallas kernels for 4%

profile of v3, /device:TPU:1, one launch (start us, length us, event | category | flops | bytes accessed | tf_op | source)
XLA Modules:
  0.0 87.2 jit_solution(4704865268996466940)
XLA Ops:
  0.6 0.0 copy-start.2
  0.6 0.0 copy-start.3
  0.7 0.0 copy-start.1
  0.7 1.9 %broadcast_in_dim.11 = bf16[32,64,256]{2,1,0:T(8,128)(2,1)} broadcast(bf16[64,256]{1,0:T(8,128)(2,1)} %param.6), dimensions={1,2} | broadcast | bytes 1081344 | tf_op jit(solution)/shard_map/broadcast_in_dim | solution.py:109
  2.5 10.6 %all-to-all-start = ((bf16[32,64,256]{2,1,0:T(8,128)(2,1)}), bf16[32,64,256]{2,1,0:T(8,128)(2,1)S(1)}, u32[]{:S(2)}, u32[]{:S(2)}) async-start(bf16[32,64,256]{2,1,0:T(8,128)(2,1)} %broadcast_in_dim.11), calls=%async_computation | async-start | bytes 2097152 | tf_op jit(solution)/shard_map/all_to_all | solution.py:108
  13.1 0.0 copy-done.2
  13.2 0.1 pad.24.clone
  13.3 0.0 copy-done.3
  13.3 0.0 copy-done.1
  13.3 0.1 maximum_maximum_fusion
  13.4 34.7 %all-gather = bf16[1280,256]{1,0:T(8,128)(2,1)S(1)} all-gather(bf16[80,256]{1,0:T(8,128)(2,1)S(1)} %maximum_maximum_fusion), channel_id=2, replica_groups={{256,292,320,356,384,420,448,484,0,36,64,100,128,164,192,228},{260,288,..., dimensions={0}, use_global_device_ids=true | all-gather | bytes 696320 | tf_op jit(solution)/shard_map/all_gather | solution.py:123
  48.2 0.0 all-to-all-done
  48.2 0.8 broadcast_in_dim.10
  49.0 4.1 %all-to-all-start.1 = ((bf16[4,16,3328]{2,1,0:T(8,128)(2,1)}), bf16[4,16,3328]{2,1,0:T(8,128)(2,1)}, u32[]{:S(2)}, u32[]{:S(2)}) async-start(bf16[4,16,3328]{2,1,0:T(8,128)(2,1)} %broadcast_in_dim.10), calls=%async_computation.1 | async-start | bytes 851968 | tf_op jit(solution)/shard_map/all_to_all | solution.py:128
  53.1 0.1 pad_add_fusion.refs_0_
  53.2 0.0 copy-start
  53.2 3.4 %partial_lse.1.refs_4_ = f32[16,128]{1,0:T(8,128)S(1)} custom-call(bf16[16,80,256]{2,1,0:T(8,128)(2,1)S(1)} %bitcast.42, bf16[2048,256]{1,0:T(8,128)(2,1)S(1)} %bitcast.39), custom_call_target="tpu_custom_call" | custom-call | flops 536870912 | bytes 2097152 | tf_op jit(solution)/shard_map/partial_lse/pallas_call | solution.py:133
  56.6 4.1 %all-to-all-done.1 = bf16[4,16,3328]{2,1,0:T(8,128)(2,1)} async-done(((bf16[4,16,3328]{2,1,0:T(8,128)(2,1)}), bf16[4,16,3328]{2,1,0:T(8,128)(2,1)}, u32[]{:S(2)}, u32[]{:S(2)}) %all-to-all-start.1) | async-done | bytes 426016 | tf_op jit(solution)/shard_map/all_to_all | solution.py:128
  60.7 4.1 %all_gather.11.refs_1_ = bf16[128,3328]{1,0:T(8,128)(2,1)S(1)} all-gather(bf16[64,3328]{1,0:T(8,128)(2,1)} %bitcast.11), channel_id=1, replica_groups={{0,4},{36,32},{64,68},{100,96},{128,132},{164,160},{192,196},{228,224},..., dimensions={0}, use_global_device_ids=true | all-gather | bytes 1277952 | tf_op jit(solution)/shard_map/all_gather | solution.py:130
  64.8 1.9 %listed_scores.1 = f32[128,128]{1,0:T(8,128)} custom-call(s32[2]{0:T(128)S(1)} %pad_add_fusion.refs_0_, bf16[128,3328]{1,0:T(8,128)(2,1)S(1)} %all_gather.11.refs_1_, bf16[2048,256]{1,0:T(8,128)(2,1)S(1)} %bitcast.40, bf16[256,2816]{1,0:T(8,128)(2,1)S(1)} %copy-done, f32[16,128]{1,0:T(8,128)S(1)} %partial_lse.1.refs_4_), custom_call_target="tpu_custom_call" | custom-call | flops 201326592 | bytes 3145728 | tf_op jit(solution)/shard_map/listed_scores/pallas_call | solution.py:150
  66.7 14.3 %all-to-all-start.2 = ((f32[128,1,128]{2,1,0:T(1,128)}), f32[128,1,128]{2,1,0:T(1,128)S(1)}, u32[]{:S(2)}, u32[]{:S(2)}) async-start(f32[128,1,128]{2,1,0:T(1,128)} %bitcast.13), calls=%async_computation.2 | async-start | bytes 131072 | tf_op jit(solution)/shard_map/all_to_all | solution.py:161
  81.7 0.2 fusion.1
  81.9 4.6 %all-to-all-done.2 = f32[128,1,128]{2,1,0:T(1,128)S(1)} async-done(((f32[128,1,128]{2,1,0:T(1,128)}), f32[128,1,128]{2,1,0:T(1,128)S(1)}, u32[]{:S(2)}, u32[]{:S(2)}) %all-to-all-start.2) | async-done | bytes 65568 | tf_op jit(solution)/shard_map/all_to_all | solution.py:161
  86.5 0.7 finish.1
  (12 shorter events, 0.2 us)
Async XLA Ops:
  0.6 12.5 %copy-start.2 = (bf16[1,3072]{1,0:T(2,128)(2,1)S(1)}, bf16[1,3072]{1,0:T(2,128)(2,1)}, u32[]{:S(2)}) copy-start(bf16[1,3072]{1,0:T(2,128)(2,1)} %param.9) | copy-start | bytes 18436
  0.6 12.6 %copy-start.3 = (s32[1,100]{1,0:T(1,128)S(1)}, s32[1,100]{1,0:T(1,128)}, u32[]{:S(2)}) copy-start(s32[1,100]{1,0:T(1,128)} %param.10) | copy-start | bytes 1204
  0.7 12.6 %copy-start.1 = (bf16[64,256]{1,0:T(8,128)(2,1)S(1)}, bf16[64,256]{1,0:T(8,128)(2,1)}, u32[]{:S(2)}) copy-start(bf16[64,256]{1,0:T(8,128)(2,1)} %param.8) | copy-start | bytes 98308
  2.5 45.6 %all-to-all-start = ((bf16[32,64,256]{2,1,0:T(8,128)(2,1)}), bf16[32,64,256]{2,1,0:T(8,128)(2,1)S(1)}, u32[]{:S(2)}, u32[]{:S(2)}) async-start(bf16[32,64,256]{2,1,0:T(8,128)(2,1)} %broadcast_in_dim.11), calls=%async_computation | async-start | bytes 2097152 | tf_op jit(solution)/shard_map/all_to_all | solution.py:108
  49.0 11.8 %all-to-all-start.1 = ((bf16[4,16,3328]{2,1,0:T(8,128)(2,1)}), bf16[4,16,3328]{2,1,0:T(8,128)(2,1)}, u32[]{:S(2)}, u32[]{:S(2)}) async-start(bf16[4,16,3328]{2,1,0:T(8,128)(2,1)} %broadcast_in_dim.10), calls=%async_computation.1 | async-start | bytes 851968 | tf_op jit(solution)/shard_map/all_to_all | solution.py:128
  53.2 11.6 %copy-start = (bf16[256,2816]{1,0:T(8,128)(2,1)S(1)}, bf16[256,2816]{1,0:T(8,128)(2,1)}, u32[]{:S(2)}) copy-start(bf16[256,2816]{1,0:T(8,128)(2,1)} %refs_3_.1) | copy-start | bytes 4325380
  66.7 19.8 %all-to-all-start.2 = ((f32[128,1,128]{2,1,0:T(1,128)}), f32[128,1,128]{2,1,0:T(1,128)S(1)}, u32[]{:S(2)}, u32[]{:S(2)}) async-start(f32[128,1,128]{2,1,0:T(1,128)} %bitcast.13), calls=%async_computation.2 | async-start | bytes 131072 | tf_op jit(solution)/shard_map/all_to_all | solution.py:161

commit v4 on v3

--- a/solution.py
+++ b/solution.py
@@ -119,7 +119,8 @@
             jnp.zeros((-extra % 16, head), queries_now.dtype),
         ]
     )
-    rings = [[z * cores + (z + ring) % cores for z in around] for ring in range(cores)]
+    orders = [around, around[::-1]]
+    rings = [[z * cores + (z + ring) % cores for z in orders[ring]] for ring in range(cores)]
     column = lax.all_gather(sent, PAIR, axis_index_groups=rings)
     asked = column[:, own_rows : own_rows + extra].reshape(depth, extra * head)
 
@@ -157,11 +158,12 @@
         name="listed_scores",
     )(jnp.stack([core * ys + y, z * plane + place]), asked, passages, tails, parts)
 
-    groups = [z * plane + i * cores + (z + ring) % cores for ring in range(cores) for i in range(ys) for z in around]
+    groups = [z * plane + i * cores + (z + ring) % cores for ring in range(cores) for i in range(ys) for z in orders[ring]]
     back = lax.all_to_all(merged, BACK, 0, 0, tiled=True, axis_index_groups=[groups])
 
     far = shard // plane
-    row = ((shard + far) % cores * ys + shard // cores % ys) * depth + (far + turn) % depth
+    ring, at = (shard + far) % cores, (far + turn) % depth
+    row = (ring * ys + shard // cores % ys) * depth + jnp.where(ring == 0, at, depth - 1 - at)
     before = jnp.arange(count)[:, None] > jnp.arange(count)[None, :]
     second = jnp.any((shard[:, None] == shard[None, :]) & before, axis=1).astype(jnp.int32)
     lse_now, rerank = pl.pallas_call(

time: 87.6 us -> 86.4 us (0.986)
  waiting for transfers between devices: 8.75 us -> 7.71 us
    all_gather x1, blocking collectives: 34.7 us -> 33.3 us  [local(): column = lax.all_gather(sent, PAIR, axis_index_groups=rings)]
    all_gather x1, blocking collectives: 4.08 us -> 5.25 us  [local(): asked = lax.all_gather(asked, PAIR, tiled=True, axis_index_groups=pairs)]
    all_to_all x1, waiting for transfers between devices: 4.09 us -> 2.97 us  [local(): lax.all_to_all(asked, 'y', 0, 0, tiled=True).reshape(-1, extra * head)]
where the time goes in v4:
time: 86.4 us; the launch traced here: 86 us
  blocking collectives  38.6 us (45%)
  starting transfers between devices  29 us (34%)
  waiting for transfers between devices  7.71 us (9%)
  Pallas kernels  5.99 us (7%)
  local copies, waits for them, and re-layouts  2.82 us (3%)
  between operations  1.45 us (2%)
    all_gather x1, blocking collectives, local(): column = lax.all_gather(sent, PAIR, axis_index_groups=rings)  33.3 us
    all_to_all x1, starting transfers between devices, local(): lax.all_to_all(merged, BACK, 0, 0, tiled=True, axis_index_groups=[groups])  14.3 us
    all_to_all x1, starting transfers between devices, local(): lax.all_to_all(jnp.broadcast_to(prefixes[None], (plane * lax.axis_size('x...  10.6 us
    all_gather x1, blocking collectives, local(): asked = lax.all_gather(asked, PAIR, tiled=True, axis_index_groups=pairs)  5.25 us
    all_to_all x1, waiting for transfers between devices, local(): lax.all_to_all(merged, BACK, 0, 0, tiled=True, axis_index_groups=[groups])  4.73 us
    all_to_all x1, starting transfers between devices, local(): lax.all_to_all(asked, 'y', 0, 0, tiled=True).reshape(-1, extra * head)  4.12 us
    pallas_call x1, Pallas kernels, local(): pl.pallas_call(lambda *refs: partial_lse(head ** (-0.5), own_rows, *refs)...  3.45 us
    all_to_all x1, waiting for transfers between devices, local(): lax.all_to_all(asked, 'y', 0, 0, tiled=True).reshape(-1, extra * head)  2.97 us
  transfers between devices with their start and end apart: 3, of which 2 were waited for; matrix products, arithmetic and copies ran while one was open for 1% of the time, Pallas kernels for 4%

profile of v4, /device:TPU:1, one launch (start us, length us, event | category | flops | bytes accessed | tf_op | source)
XLA Modules:
  0.0 86.0 jit_solution(6967323066636929822)
XLA Ops:
  0.6 0.0 copy-start.2
  0.6 0.0 copy-start.3
  0.7 0.0 copy-start.1
  0.7 1.9 %broadcast_in_dim.11 = bf16[32,64,256]{2,1,0:T(8,128)(2,1)} broadcast(bf16[64,256]{1,0:T(8,128)(2,1)} %param.6), dimensions={1,2} | broadcast | bytes 1081344 | tf_op jit(solution)/shard_map/broadcast_in_dim | solution.py:109
  2.5 10.6 %all-to-all-start = ((bf16[32,64,256]{2,1,0:T(8,128)(2,1)}), bf16[32,64,256]{2,1,0:T(8,128)(2,1)S(1)}, u32[]{:S(2)}, u32[]{:S(2)}) async-start(bf16[32,64,256]{2,1,0:T(8,128)(2,1)} %broadcast_in_dim.11), calls=%async_computation | async-start | bytes 2097152 | tf_op jit(solution)/shard_map/all_to_all | solution.py:108
  13.1 0.0 copy-done.2
  13.2 0.1 pad.24.clone
  13.3 0.0 copy-done.3
  13.3 0.1 maximum_maximum_fusion
  13.4 33.3 %all-gather = bf16[1280,256]{1,0:T(8,128)(2,1)S(1)} all-gather(bf16[80,256]{1,0:T(8,128)(2,1)S(1)} %maximum_maximum_fusion), channel_id=2, replica_groups={{256,292,320,356,384,420,448,484,0,36,64,100,128,164,192,228},{224,196,..., dimensions={0}, use_global_device_ids=true | all-gather | bytes 696320 | tf_op jit(solution)/shard_map/all_gather | solution.py:124
  46.8 0.0 all-to-all-done
  46.8 0.8 broadcast_in_dim.10
  47.6 4.1 %all-to-all-start.1 = ((bf16[4,16,3328]{2,1,0:T(8,128)(2,1)}), bf16[4,16,3328]{2,1,0:T(8,128)(2,1)}, u32[]{:S(2)}, u32[]{:S(2)}) async-start(bf16[4,16,3328]{2,1,0:T(8,128)(2,1)} %broadcast_in_dim.10), calls=%async_computation.1 | async-start | bytes 851968 | tf_op jit(solution)/shard_map/all_to_all | solution.py:129
  51.7 0.1 pad_add_fusion.refs_0_
  51.8 0.0 copy-start
  51.8 3.4 %partial_lse.1.refs_4_ = f32[16,128]{1,0:T(8,128)S(1)} custom-call(bf16[16,80,256]{2,1,0:T(8,128)(2,1)S(1)} %bitcast.42, bf16[2048,256]{1,0:T(8,128)(2,1)S(1)} %bitcast.39), custom_call_target="tpu_custom_call" | custom-call | flops 536870912 | bytes 2097152 | tf_op jit(solution)/shard_map/partial_lse/pallas_call | solution.py:134
  55.3 3.0 %all-to-all-done.1 = bf16[4,16,3328]{2,1,0:T(8,128)(2,1)} async-done(((bf16[4,16,3328]{2,1,0:T(8,128)(2,1)}), bf16[4,16,3328]{2,1,0:T(8,128)(2,1)}, u32[]{:S(2)}, u32[]{:S(2)}) %all-to-all-start.1) | async-done | bytes 426016 | tf_op jit(solution)/shard_map/all_to_all | solution.py:129
  58.3 5.3 %all_gather.11.refs_1_ = bf16[128,3328]{1,0:T(8,128)(2,1)S(1)} all-gather(bf16[64,3328]{1,0:T(8,128)(2,1)} %bitcast.11), channel_id=1, replica_groups={{0,4},{36,32},{64,68},{100,96},{128,132},{164,160},{192,196},{228,224},..., dimensions={0}, use_global_device_ids=true | all-gather | bytes 1277952 | tf_op jit(solution)/shard_map/all_gather | solution.py:131
  63.5 0.0 copy-done
  63.5 1.9 %listed_scores.1 = f32[128,128]{1,0:T(8,128)} custom-call(s32[2]{0:T(128)S(1)} %pad_add_fusion.refs_0_, bf16[128,3328]{1,0:T(8,128)(2,1)S(1)} %all_gather.11.refs_1_, bf16[2048,256]{1,0:T(8,128)(2,1)S(1)} %bitcast.40, bf16[256,2816]{1,0:T(8,128)(2,1)S(1)} %copy-done, f32[16,128]{1,0:T(8,128)S(1)} %partial_lse.1.refs_4_), custom_call_target="tpu_custom_call" | custom-call | flops 201326592 | bytes 3145728 | tf_op jit(solution)/shard_map/listed_scores/pallas_call | solution.py:151
  65.4 14.3 %all-to-all-start.2 = ((f32[128,1,128]{2,1,0:T(1,128)}), f32[128,1,128]{2,1,0:T(1,128)S(1)}, u32[]{:S(2)}, u32[]{:S(2)}) async-start(f32[128,1,128]{2,1,0:T(1,128)} %bitcast.13), calls=%async_computation.2 | async-start | bytes 131072 | tf_op jit(solution)/shard_map/all_to_all | solution.py:162
  80.4 0.2 fusion.1
  80.6 4.7 %all-to-all-done.2 = f32[128,1,128]{2,1,0:T(1,128)S(1)} async-done(((f32[128,1,128]{2,1,0:T(1,128)}), f32[128,1,128]{2,1,0:T(1,128)S(1)}, u32[]{:S(2)}, u32[]{:S(2)}) %all-to-all-start.2) | async-done | bytes 65568 | tf_op jit(solution)/shard_map/all_to_all | solution.py:162
  85.3 0.7 finish.1
  (12 shorter events, 0.2 us)
Async XLA Ops:
  0.6 12.5 %copy-start.2 = (bf16[1,3072]{1,0:T(2,128)(2,1)S(1)}, bf16[1,3072]{1,0:T(2,128)(2,1)}, u32[]{:S(2)}) copy-start(bf16[1,3072]{1,0:T(2,128)(2,1)} %param.9) | copy-start | bytes 18436
  0.6 12.6 %copy-start.3 = (s32[1,100]{1,0:T(1,128)S(1)}, s32[1,100]{1,0:T(1,128)}, u32[]{:S(2)}) copy-start(s32[1,100]{1,0:T(1,128)} %param.10) | copy-start | bytes 1204
  0.7 12.6 %copy-start.1 = (bf16[64,256]{1,0:T(8,128)(2,1)S(1)}, bf16[64,256]{1,0:T(8,128)(2,1)}, u32[]{:S(2)}) copy-start(bf16[64,256]{1,0:T(8,128)(2,1)} %param.8) | copy-start | bytes 98308
  2.5 44.3 %all-to-all-start = ((bf16[32,64,256]{2,1,0:T(8,128)(2,1)}), bf16[32,64,256]{2,1,0:T(8,128)(2,1)S(1)}, u32[]{:S(2)}, u32[]{:S(2)}) async-start(bf16[32,64,256]{2,1,0:T(8,128)(2,1)} %broadcast_in_dim.11), calls=%async_computation | async-start | bytes 2097152 | tf_op jit(solution)/shard_map/all_to_all | solution.py:108
  47.6 10.7 %all-to-all-start.1 = ((bf16[4,16,3328]{2,1,0:T(8,128)(2,1)}), bf16[4,16,3328]{2,1,0:T(8,128)(2,1)}, u32[]{:S(2)}, u32[]{:S(2)}) async-start(bf16[4,16,3328]{2,1,0:T(8,128)(2,1)} %broadcast_in_dim.10), calls=%async_computation.1 | async-start | bytes 851968 | tf_op jit(solution)/shard_map/all_to_all | solution.py:129
  51.8 11.7 %copy-start = (bf16[256,2816]{1,0:T(8,128)(2,1)S(1)}, bf16[256,2816]{1,0:T(8,128)(2,1)}, u32[]{:S(2)}) copy-start(bf16[256,2816]{1,0:T(8,128)(2,1)} %refs_3_.1) | copy-start | bytes 4325380
  65.4 19.9 %all-to-all-start.2 = ((f32[128,1,128]{2,1,0:T(1,128)}), f32[128,1,128]{2,1,0:T(1,128)S(1)}, u32[]{:S(2)}, u32[]{:S(2)}) async-start(f32[128,1,128]{2,1,0:T(1,128)} %bitcast.13), calls=%async_computation.2 | async-start | bytes 131072 | tf_op jit(solution)/shard_map/all_to_all | solution.py:162

commit v5 on v4

--- a/solution.py
+++ b/solution.py
@@ -46,10 +46,12 @@
         out_ref[pl.ds(first + group, 1), :rows] = found[:, group * rows : (group + 1) * rows]
 
 
-def listed_scores(rows, place_ref, asked_ref, prefixes_ref, tails_ref, parts_ref, out_ref):
+def listed_scores(rows, asked_ref, prefixes_ref, tails_ref, parts_ref, out_ref):
     shard_rows, head = tails_ref.shape[0], prefixes_ref.shape[1]
     full = head + tails_ref.shape[1]
-    start = pl.multiple_of(place_ref[0] * shard_rows, shard_rows)
+    z, y, core = lax.axis_index("z"), lax.axis_index("y"), lax.axis_index("core")
+    ys, cores = lax.axis_size("y"), lax.axis_size("core")
+    start = pl.multiple_of((core * ys + y) * shard_rows, shard_rows)
     dims = (((1,), (1,)), ((), ()))
     scores = lax.dot_general(
         asked_ref[:, :head], prefixes_ref[pl.ds(start, shard_rows), :], dims, preferred_element_type=jnp.float32
@@ -58,7 +60,7 @@
     shards = asked_ref[:, full : full + LANES].astype(jnp.float32)
     offsets = asked_ref[:, full + LANES : full + 2 * LANES].astype(jnp.float32)
     lanes = lax.broadcasted_iota(jnp.int32, (count, LANES), 1)
-    mine = shards == place_ref[1].astype(jnp.float32)
+    mine = shards == ((z * ys + y) * cores + core).astype(jnp.float32)
     key = lanes.astype(jnp.float32) * shard_rows + offsets
     low = jnp.min(jnp.where(mine, key, float(LANES * shard_rows)), axis=1, keepdims=True)
     high = jnp.max(jnp.where(mine, key, 0.0), axis=1, keepdims=True)
@@ -73,9 +75,11 @@
     out_ref[...] = jnp.where(lanes < rows, parts, jnp.where(lanes == rows, pick(low), pick(high)))
 
 
-def finish(scale, rows, depth, own_ref, row_ref, second_ref, back_ref, prev_ref, lse_ref, rerank_ref):
+def finish(scale, rows, depth, row_ref, second_ref, back_ref, prev_ref, lse_ref, rerank_ref):
     count = rerank_ref.shape[1]
-    start = pl.multiple_of(own_ref[0] * depth, depth)
+    cores = lax.axis_size("core")
+    ring = (lax.axis_index("z") + lax.axis_index("core")) % cores
+    start = pl.multiple_of((ring * lax.axis_size("y") + lax.axis_index("y")) * depth, depth)
     parts = back_ref[pl.ds(start, depth), :rows]
     peak = jnp.max(parts, axis=0, keepdims=True)
     lse_ref[...] = peak + jnp.log(jnp.sum(jnp.exp(parts - peak), axis=0, keepdims=True))
@@ -147,16 +151,15 @@
     )(column, passages)
 
     z, y, core = lax.axis_index("z"), lax.axis_index("y"), lax.axis_index("core")
-    place = y * cores + core
     merged = pl.pallas_call(
         lambda *refs: listed_scores(own_rows, *refs),
-        in_specs=[smem, vmem, vmem, vmem, vmem],
+        in_specs=[vmem, vmem, vmem, vmem],
         out_specs=vmem,
         out_shape=jax.ShapeDtypeStruct((plane * depth, LANES), jnp.float32),
         compiler_params=pltpu.CompilerParams(vmem_limit_bytes=32 * 2**20),
         cost_estimate=pl.CostEstimate(flops=2 * 128 * 256 * 3072, bytes_accessed=3 * 2**20, transcendentals=0),
         name="listed_scores",
-    )(jnp.stack([core * ys + y, z * plane + place]), asked, passages, tails, parts)
+    )(asked, passages, tails, parts)
 
     groups = [z * plane + i * cores + (z + ring) % cores for ring in range(cores) for i in range(ys) for z in orders[ring]]
     back = lax.all_to_all(merged, BACK, 0, 0, tiled=True, axis_index_groups=[groups])
@@ -168,7 +171,7 @@
     second = jnp.any((shard[:, None] == shard[None, :]) & before, axis=1).astype(jnp.int32)
     lse_now, rerank = pl.pallas_call(
         lambda *refs: finish(full_width**-0.5, own_rows, depth, *refs),
-        in_specs=[smem, vmem, vmem, vmem, smem],
+        in_specs=[vmem, vmem, vmem, smem],
         out_specs=[vmem, vmem],
         out_shape=[
             jax.ShapeDtypeStruct((1, own_rows), jnp.float32),
@@ -177,7 +180,6 @@
         compiler_params=pltpu.CompilerParams(vmem_limit_bytes=32 * 2**20),
         name="finish",
     )(
-        ((core + z) % cores * ys + y).reshape(1),
         jnp.pad(row, (0, LANES - count)).reshape(1, LANES),
         jnp.pad(second, (0, LANES - count)).reshape(1, LANES),
         back,

time: 86.4 us -> 85.8 us (level)
  no operation moved by 1% of the time
where the time goes in v5:
time: 85.8 us; the launch traced here: 85.4 us
  blocking collectives  38.6 us (45%)
  starting transfers between devices  29 us (34%)
  waiting for transfers between devices  7.77 us (9%)
  Pallas kernels  5.45 us (6%)
  local copies, waits for them, and re-layouts  2.82 us (3%)
  between operations  1.44 us (2%)
    all_gather x1, blocking collectives, local(): column = lax.all_gather(sent, PAIR, axis_index_groups=rings)  33.3 us
    all_to_all x1, starting transfers between devices, local(): lax.all_to_all(merged, BACK, 0, 0, tiled=True, axis_index_groups=[groups])  14.3 us
    all_to_all x1, starting transfers between devices, local(): lax.all_to_all(jnp.broadcast_to(prefixes[None], (plane * lax.axis_size('x...  10.6 us
    all_gather x1, blocking collectives, local(): asked = lax.all_gather(asked, PAIR, tiled=True, axis_index_groups=pairs)  5.25 us
    all_to_all x1, waiting for transfers between devices, local(): lax.all_to_all(merged, BACK, 0, 0, tiled=True, axis_index_groups=[groups])  4.74 us
    all_to_all x1, starting transfers between devices, local(): lax.all_to_all(asked, 'y', 0, 0, tiled=True).reshape(-1, extra * head)  4.12 us
    pallas_call x1, Pallas kernels, local(): pl.pallas_call(lambda *refs: partial_lse(head ** (-0.5), own_rows, *refs)...  3.45 us
    all_to_all x1, waiting for transfers between devices, local(): lax.all_to_all(asked, 'y', 0, 0, tiled=True).reshape(-1, extra * head)  3.03 us
  transfers between devices with their start and end apart: 3, of which 2 were waited for; matrix products, arithmetic and copies ran while one was open for 1% of the time, Pallas kernels for 4%

profile of v5, /device:TPU:1, one launch (start us, length us, event | category | flops | bytes accessed | tf_op | source)
XLA Modules:
  0.0 85.4 jit_solution(7244190022530030830)
XLA Ops:
  0.6 0.0 copy-start.2
  0.6 0.0 copy-start.3
  0.7 0.0 copy-start.1
  0.7 1.9 %broadcast_in_dim.11 = bf16[32,64,256]{2,1,0:T(8,128)(2,1)} broadcast(bf16[64,256]{1,0:T(8,128)(2,1)} %param.6), dimensions={1,2} | broadcast | bytes 1081344 | tf_op jit(solution)/shard_map/broadcast_in_dim | solution.py:113
  2.5 10.6 %all-to-all-start = ((bf16[32,64,256]{2,1,0:T(8,128)(2,1)}), bf16[32,64,256]{2,1,0:T(8,128)(2,1)S(1)}, u32[]{:S(2)}, u32[]{:S(2)}) async-start(bf16[32,64,256]{2,1,0:T(8,128)(2,1)} %broadcast_in_dim.11), calls=%async_computation | async-start | bytes 2097152 | tf_op jit(solution)/shard_map/all_to_all | solution.py:112
  13.1 0.0 copy-done.2
  13.2 0.1 pad.24.clone
  13.2 0.0 copy-done.3
  13.3 0.0 copy-done.1
  13.3 0.1 maximum_maximum_fusion
  13.4 33.3 %all-gather = bf16[1280,256]{1,0:T(8,128)(2,1)S(1)} all-gather(bf16[80,256]{1,0:T(8,128)(2,1)S(1)} %maximum_maximum_fusion), channel_id=2, replica_groups={{256,292,320,356,384,420,448,484,0,36,64,100,128,164,192,228},{224,196,..., dimensions={0}, use_global_device_ids=true | all-gather | bytes 696320 | tf_op jit(solution)/shard_map/all_gather | solution.py:128
  46.8 0.0 all-to-all-done
  46.8 0.8 broadcast_in_dim.10
  47.6 4.1 %all-to-all-start.1 = ((bf16[4,16,3328]{2,1,0:T(8,128)(2,1)}), bf16[4,16,3328]{2,1,0:T(8,128)(2,1)}, u32[]{:S(2)}, u32[]{:S(2)}) async-start(bf16[4,16,3328]{2,1,0:T(8,128)(2,1)} %broadcast_in_dim.10), calls=%async_computation.1 | async-start | bytes 851968 | tf_op jit(solution)/shard_map/all_to_all | solution.py:133
  51.7 0.0 copy-start
  51.7 3.4 %partial_lse.1.refs_3_ = f32[16,128]{1,0:T(8,128)S(1)} custom-call(bf16[16,80,256]{2,1,0:T(8,128)(2,1)S(1)} %bitcast.39, bf16[2048,256]{1,0:T(8,128)(2,1)S(1)} %bitcast.36), custom_call_target="tpu_custom_call" | custom-call | flops 536870912 | bytes 2097152 | tf_op jit(solution)/shard_map/partial_lse/pallas_call | solution.py:138
  55.2 3.0 %all-to-all-done.1 = bf16[4,16,3328]{2,1,0:T(8,128)(2,1)} async-done(((bf16[4,16,3328]{2,1,0:T(8,128)(2,1)}), bf16[4,16,3328]{2,1,0:T(8,128)(2,1)}, u32[]{:S(2)}, u32[]{:S(2)}) %all-to-all-start.1) | async-done | bytes 426016 | tf_op jit(solution)/shard_map/all_to_all | solution.py:133
  58.2 5.3 %all_gather.11.refs_0_ = bf16[128,3328]{1,0:T(8,128)(2,1)S(1)} all-gather(bf16[64,3328]{1,0:T(8,128)(2,1)} %bitcast.8), channel_id=1, replica_groups={{0,4},{36,32},{64,68},{100,96},{128,132},{164,160},{192,196},{228,224},..., dimensions={0}, use_global_device_ids=true | all-gather | bytes 1277952 | tf_op jit(solution)/shard_map/all_gather | solution.py:135
  63.5 0.0 copy-done
  63.5 1.3 %listed_scores.1 = f32[128,128]{1,0:T(8,128)} custom-call(bf16[128,3328]{1,0:T(8,128)(2,1)S(1)} %all_gather.11.refs_0_, bf16[2048,256]{1,0:T(8,128)(2,1)S(1)} %bitcast.37, bf16[256,2816]{1,0:T(8,128)(2,1)S(1)} %copy-done, f32[16,128]{1,0:T(8,128)S(1)} %partial_lse.1.refs_3_), custom_call_target="tpu_custom_call" | custom-call | flops 201326592 | bytes 3145728 | tf_op jit(solution)/shard_map/listed_scores/pallas_call | solution.py:154
  64.8 14.3 %all-to-all-start.2 = ((f32[128,1,128]{2,1,0:T(1,128)}), f32[128,1,128]{2,1,0:T(1,128)S(1)}, u32[]{:S(2)}, u32[]{:S(2)}) async-start(f32[128,1,128]{2,1,0:T(1,128)} %bitcast.10), calls=%async_computation.2 | async-start | bytes 131072 | tf_op jit(solution)/shard_map/all_to_all | solution.py:165
  79.1 0.2 fusion.1
  80.0 4.7 %all-to-all-done.2 = f32[128,1,128]{2,1,0:T(1,128)S(1)} async-done(((f32[128,1,128]{2,1,0:T(1,128)}), f32[128,1,128]{2,1,0:T(1,128)S(1)}, u32[]{:S(2)}, u32[]{:S(2)}) %all-to-all-start.2) | async-done | bytes 65568 | tf_op jit(solution)/shard_map/all_to_all | solution.py:165
  84.7 0.7 finish.1
  (11 shorter events, 0.2 us)
Async XLA Ops:
  0.6 12.5 %copy-start.2 = (bf16[1,3072]{1,0:T(2,128)(2,1)S(1)}, bf16[1,3072]{1,0:T(2,128)(2,1)}, u32[]{:S(2)}) copy-start(bf16[1,3072]{1,0:T(2,128)(2,1)} %param.9) | copy-start | bytes 18436
  0.6 12.6 %copy-start.3 = (s32[1,100]{1,0:T(1,128)S(1)}, s32[1,100]{1,0:T(1,128)}, u32[]{:S(2)}) copy-start(s32[1,100]{1,0:T(1,128)} %param.10) | copy-start | bytes 1204
  0.7 12.6 %copy-start.1 = (bf16[64,256]{1,0:T(8,128)(2,1)S(1)}, bf16[64,256]{1,0:T(8,128)(2,1)}, u32[]{:S(2)}) copy-start(bf16[64,256]{1,0:T(8,128)(2,1)} %param.8) | copy-start | bytes 98308
  2.5 44.2 %all-to-all-start = ((bf16[32,64,256]{2,1,0:T(8,128)(2,1)}), bf16[32,64,256]{2,1,0:T(8,128)(2,1)S(1)}, u32[]{:S(2)}, u32[]{:S(2)}) async-start(bf16[32,64,256]{2,1,0:T(8,128)(2,1)} %broadcast_in_dim.11), calls=%async_computation | async-start | bytes 2097152 | tf_op jit(solution)/shard_map/all_to_all | solution.py:112
  47.6 10.7 %all-to-all-start.1 = ((bf16[4,16,3328]{2,1,0:T(8,128)(2,1)}), bf16[4,16,3328]{2,1,0:T(8,128)(2,1)}, u32[]{:S(2)}, u32[]{:S(2)}) async-start(bf16[4,16,3328]{2,1,0:T(8,128)(2,1)} %broadcast_in_dim.10), calls=%async_computation.1 | async-start | bytes 851968 | tf_op jit(solution)/shard_map/all_to_all | solution.py:133
  51.7 11.8 %copy-start = (bf16[256,2816]{1,0:T(8,128)(2,1)S(1)}, bf16[256,2816]{1,0:T(8,128)(2,1)}, u32[]{:S(2)}) copy-start(bf16[256,2816]{1,0:T(8,128)(2,1)} %refs_2_.1) | copy-start | bytes 4325380
  64.8 19.9 %all-to-all-start.2 = ((f32[128,1,128]{2,1,0:T(1,128)}), f32[128,1,128]{2,1,0:T(1,128)S(1)}, u32[]{:S(2)}, u32[]{:S(2)}) async-start(f32[128,1,128]{2,1,0:T(1,128)} %bitcast.10), calls=%async_computation.2 | async-start | bytes 131072 | tf_op jit(solution)/shard_map/all_to_all | solution.py:165

commit v6 on v5

--- a/solution.py
+++ b/solution.py
@@ -43,7 +43,7 @@
         out_ref[...] = jnp.zeros_like(out_ref)
 
     for group in range(groups):
-        out_ref[pl.ds(first + group, 1), :rows] = found[:, group * rows : (group + 1) * rows]
+        out_ref[pl.ds(first + group, 1), LANES - rows :] = found[:, group * rows : (group + 1) * rows]
 
 
 def listed_scores(rows, asked_ref, prefixes_ref, tails_ref, parts_ref, out_ref):
@@ -54,25 +54,26 @@
     start = pl.multiple_of((core * ys + y) * shard_rows, shard_rows)
     dims = (((1,), (1,)), ((), ()))
     scores = lax.dot_general(
-        asked_ref[:, :head], prefixes_ref[pl.ds(start, shard_rows), :], dims, preferred_element_type=jnp.float32
-    ) + lax.dot_general(asked_ref[:, head:full], tails_ref[...], dims, preferred_element_type=jnp.float32)
-    count = asked_ref.shape[0]
-    shards = asked_ref[:, full : full + LANES].astype(jnp.float32)
-    offsets = asked_ref[:, full + LANES : full + 2 * LANES].astype(jnp.float32)
-    lanes = lax.broadcasted_iota(jnp.int32, (count, LANES), 1)
+        prefixes_ref[pl.ds(start, shard_rows), :], asked_ref[:, :head], dims, preferred_element_type=jnp.float32
+    ) + lax.dot_general(tails_ref[...], asked_ref[:, head:full], dims, preferred_element_type=jnp.float32)
+    count, depth = asked_ref.shape[0], parts_ref.shape[0]
+    shards = asked_ref[:, full : full + LANES].astype(jnp.float32).T
+    offsets = asked_ref[:, full + LANES : full + 2 * LANES].astype(jnp.float32).T
     mine = shards == ((z * ys + y) * cores + core).astype(jnp.float32)
-    key = lanes.astype(jnp.float32) * shard_rows + offsets
-    low = jnp.min(jnp.where(mine, key, float(LANES * shard_rows)), axis=1, keepdims=True)
-    high = jnp.max(jnp.where(mine, key, 0.0), axis=1, keepdims=True)
-    column = lax.broadcasted_iota(jnp.int32, scores.shape, 1)
+    key = lax.broadcasted_iota(jnp.int32, shards.shape, 0).astype(jnp.float32) * shard_rows + offsets
+    low = jnp.min(jnp.where(mine, key, float(LANES * shard_rows)), axis=0, keepdims=True)
+    high = jnp.max(jnp.where(mine, key, 0.0), axis=0, keepdims=True)
+    row = lax.broadcasted_iota(jnp.int32, scores.shape, 0)
 
     def pick(at):
         at = (at - jnp.floor(at * (1.0 / shard_rows)) * shard_rows).astype(jnp.int32)
-        return jnp.sum(jnp.where(column == at, scores, 0.0), axis=1, keepdims=True)
-
-    depth = parts_ref.shape[0]
-    parts = jnp.concatenate([parts_ref[...]] * (count // depth), axis=0)
-    out_ref[...] = jnp.where(lanes < rows, parts, jnp.where(lanes == rows, pick(low), pick(high)))
+        return jnp.sum(jnp.where(row == at, scores, 0.0), axis=0, keepdims=True)
+
+    slots = lax.broadcasted_iota(jnp.int32, (8, count), 0)
+    values = jnp.where(slots == 0, pick(low), jnp.where(slots == 1, pick(high), 0.0))
+    values = jnp.concatenate([values, jnp.zeros((LANES - 8, count), jnp.float32)], axis=0).T
+    lanes = lax.broadcasted_iota(jnp.int32, (count, LANES), 1)
+    out_ref[...] = jnp.where(lanes < 8, values, jnp.concatenate([parts_ref[...]] * (count // depth), axis=0))
 
 
 def finish(scale, rows, depth, row_ref, second_ref, back_ref, prev_ref, lse_ref, rerank_ref):
@@ -80,16 +81,16 @@
     cores = lax.axis_size("core")
     ring = (lax.axis_index("z") + lax.axis_index("core")) % cores
     start = pl.multiple_of((ring * lax.axis_size("y") + lax.axis_index("y")) * depth, depth)
-    parts = back_ref[pl.ds(start, depth), :rows]
+    parts = back_ref[pl.ds(start, depth), LANES - rows :]
     peak = jnp.max(parts, axis=0, keepdims=True)
     lse_ref[...] = peak + jnp.log(jnp.sum(jnp.exp(parts - peak), axis=0, keepdims=True))
     turned = back_ref[...].T
     shape = (8, LANES)
     at = jnp.broadcast_to(row_ref[...], shape)
-    low = jnp.take_along_axis(jnp.broadcast_to(turned[rows : rows + 1, :], shape), at, axis=1)
-    high = jnp.take_along_axis(jnp.broadcast_to(turned[rows + 1 : rows + 2, :], shape), at, axis=1)
+    low = jnp.take_along_axis(jnp.broadcast_to(turned[:1, :], shape), at, axis=1)
+    high = jnp.take_along_axis(jnp.broadcast_to(turned[1:2, :], shape), at, axis=1)
     values = jnp.where(second_ref[...] > 0, high[:1], low[:1])
-    rerank_ref[...] = values[:, :count] * scale - prev_ref[0]
+    rerank_ref[...] = values[:, :count] * scale - prev_ref[...]
 
 
 def local(prefixes, tails, queries_now, queries_prev, candidates, lse_prev):
@@ -171,7 +172,7 @@
     second = jnp.any((shard[:, None] == shard[None, :]) & before, axis=1).astype(jnp.int32)
     lse_now, rerank = pl.pallas_call(
         lambda *refs: finish(full_width**-0.5, own_rows, depth, *refs),
-        in_specs=[vmem, vmem, vmem, smem],
+        in_specs=[vmem, vmem, vmem, vmem],
         out_specs=[vmem, vmem],
         out_shape=[
             jax.ShapeDtypeStruct((1, own_rows), jnp.float32),
@@ -183,7 +184,7 @@
         jnp.pad(row, (0, LANES - count)).reshape(1, LANES),
         jnp.pad(second, (0, LANES - count)).reshape(1, LANES),
         back,
-        lse_prev,
+        lse_prev.reshape(1, 1),
     )
     return lse_now.reshape(-1), rerank
 

time: 85.8 us -> 85.8 us (level)
  no operation moved by 1% of the time
where the time goes in v6:
time: 85.8 us; the launch traced here: 85.3 us
  blocking collectives  38.6 us (45%)
  starting transfers between devices  29 us (34%)
  waiting for transfers between devices  7.77 us (9%)
  Pallas kernels  5.4 us (6%)
  local copies, waits for them, and re-layouts  2.82 us (3%)
  between operations  1.44 us (2%)
    all_gather x1, blocking collectives, local(): column = lax.all_gather(sent, PAIR, axis_index_groups=rings)  33.3 us
    all_to_all x1, starting transfers between devices, local(): lax.all_to_all(merged, BACK, 0, 0, tiled=True, axis_index_groups=[groups])  14.3 us
    all_to_all x1, starting transfers between devices, local(): lax.all_to_all(jnp.broadcast_to(prefixes[None], (plane * lax.axis_size('x...  10.6 us
    all_gather x1, blocking collectives, local(): asked = lax.all_gather(asked, PAIR, tiled=True, axis_index_groups=pairs)  5.25 us
    all_to_all x1, waiting for transfers between devices, local(): lax.all_to_all(merged, BACK, 0, 0, tiled=True, axis_index_groups=[groups])  4.74 us
    all_to_all x1, starting transfers between devices, local(): lax.all_to_all(asked, 'y', 0, 0, tiled=True).reshape(-1, extra * head)  4.12 us
    pallas_call x1, Pallas kernels, local(): pl.pallas_call(lambda *refs: partial_lse(head ** (-0.5), own_rows, *refs)...  3.45 us
    all_to_all x1, waiting for transfers between devices, local(): lax.all_to_all(asked, 'y', 0, 0, tiled=True).reshape(-1, extra * head)  3.03 us
  transfers between devices with their start and end apart: 3, of which 2 were waited for; matrix products, arithmetic and copies ran while one was open for 1% of the time, Pallas kernels for 4%

profile of v6, /device:TPU:1, one launch (start us, length us, event | category | flops | bytes accessed | tf_op | source)
XLA Modules:
  0.0 85.3 jit_solution(5570473299065150671)
XLA Ops:
  0.6 0.0 copy-start.2
  0.6 0.0 copy-start.3
  0.7 0.0 copy-start.1
  0.7 1.9 %broadcast_in_dim.11 = bf16[32,64,256]{2,1,0:T(8,128)(2,1)} broadcast(bf16[64,256]{1,0:T(8,128)(2,1)} %param.6), dimensions={1,2} | broadcast | bytes 1081344 | tf_op jit(solution)/shard_map/broadcast_in_dim | solution.py:114
  2.5 10.6 %all-to-all-start = ((bf16[32,64,256]{2,1,0:T(8,128)(2,1)}), bf16[32,64,256]{2,1,0:T(8,128)(2,1)S(1)}, u32[]{:S(2)}, u32[]{:S(2)}) async-start(bf16[32,64,256]{2,1,0:T(8,128)(2,1)} %broadcast_in_dim.11), calls=%async_computation | async-start | bytes 2097152 | tf_op jit(solution)/shard_map/all_to_all | solution.py:113
  13.1 0.0 copy-done.2
  13.2 0.1 pad.24.clone
  13.2 0.0 copy-done.3
  13.3 0.0 copy-done.1
  13.3 0.1 maximum_maximum_fusion
  13.4 33.3 %all-gather = bf16[1280,256]{1,0:T(8,128)(2,1)S(1)} all-gather(bf16[80,256]{1,0:T(8,128)(2,1)S(1)} %maximum_maximum_fusion), channel_id=2, replica_groups={{256,292,320,356,384,420,448,484,0,36,64,100,128,164,192,228},{224,196,..., dimensions={0}, use_global_device_ids=true | all-gather | bytes 696320 | tf_op jit(solution)/shard_map/all_gather | solution.py:129
  46.8 0.0 all-to-all-done
  46.8 0.8 broadcast_in_dim.10
  47.6 4.1 %all-to-all-start.1 = ((bf16[4,16,3328]{2,1,0:T(8,128)(2,1)}), bf16[4,16,3328]{2,1,0:T(8,128)(2,1)}, u32[]{:S(2)}, u32[]{:S(2)}) async-start(bf16[4,16,3328]{2,1,0:T(8,128)(2,1)} %broadcast_in_dim.10), calls=%async_computation.1 | async-start | bytes 851968 | tf_op jit(solution)/shard_map/all_to_all | solution.py:134
  51.7 0.0 copy-start
  51.7 3.4 %partial_lse.1.refs_3_ = f32[16,128]{1,0:T(8,128)S(1)} custom-call(bf16[16,80,256]{2,1,0:T(8,128)(2,1)S(1)} %bitcast.41, bf16[2048,256]{1,0:T(8,128)(2,1)S(1)} %bitcast.38), custom_call_target="tpu_custom_call" | custom-call | flops 536870912 | bytes 2097152 | tf_op jit(solution)/shard_map/partial_lse/pallas_call | solution.py:139
  55.2 3.0 %all-to-all-done.1 = bf16[4,16,3328]{2,1,0:T(8,128)(2,1)} async-done(((bf16[4,16,3328]{2,1,0:T(8,128)(2,1)}), bf16[4,16,3328]{2,1,0:T(8,128)(2,1)}, u32[]{:S(2)}, u32[]{:S(2)}) %all-to-all-start.1) | async-done | bytes 426016 | tf_op jit(solution)/shard_map/all_to_all | solution.py:134
  58.2 5.3 %all_gather.11.refs_0_ = bf16[128,3328]{1,0:T(8,128)(2,1)S(1)} all-gather(bf16[64,3328]{1,0:T(8,128)(2,1)} %bitcast.8), channel_id=1, replica_groups={{0,4},{36,32},{64,68},{100,96},{128,132},{164,160},{192,196},{228,224},..., dimensions={0}, use_global_device_ids=true | all-gather | bytes 1277952 | tf_op jit(solution)/shard_map/all_gather | solution.py:136
  63.5 0.0 copy-done
  63.5 1.3 %listed_scores.1 = f32[128,128]{1,0:T(8,128)} custom-call(bf16[128,3328]{1,0:T(8,128)(2,1)S(1)} %all_gather.11.refs_0_, bf16[2048,256]{1,0:T(8,128)(2,1)S(1)} %bitcast.39, bf16[256,2816]{1,0:T(8,128)(2,1)S(1)} %copy-done, f32[16,128]{1,0:T(8,128)S(1)} %partial_lse.1.refs_3_), custom_call_target="tpu_custom_call" | custom-call | flops 201326592 | bytes 3145728 | tf_op jit(solution)/shard_map/listed_scores/pallas_call | solution.py:155
  64.8 14.3 %all-to-all-start.2 = ((f32[128,1,128]{2,1,0:T(1,128)}), f32[128,1,128]{2,1,0:T(1,128)S(1)}, u32[]{:S(2)}, u32[]{:S(2)}) async-start(f32[128,1,128]{2,1,0:T(1,128)} %bitcast.10), calls=%async_computation.2 | async-start | bytes 131072 | tf_op jit(solution)/shard_map/all_to_all | solution.py:166
  79.1 0.2 fusion.1
  80.0 4.7 %all-to-all-done.2 = f32[128,1,128]{2,1,0:T(1,128)S(1)} async-done(((f32[128,1,128]{2,1,0:T(1,128)}), f32[128,1,128]{2,1,0:T(1,128)S(1)}, u32[]{:S(2)}, u32[]{:S(2)}) %all-to-all-start.2) | async-done | bytes 65568 | tf_op jit(solution)/shard_map/all_to_all | solution.py:166
  84.7 0.7 finish.1
  (11 shorter events, 0.2 us)
Async XLA Ops:
  0.6 12.5 %copy-start.2 = (bf16[1,3072]{1,0:T(2,128)(2,1)S(1)}, bf16[1,3072]{1,0:T(2,128)(2,1)}, u32[]{:S(2)}) copy-start(bf16[1,3072]{1,0:T(2,128)(2,1)} %param.9) | copy-start | bytes 18436
  0.6 12.6 %copy-start.3 = (s32[1,100]{1,0:T(1,128)S(1)}, s32[1,100]{1,0:T(1,128)}, u32[]{:S(2)}) copy-start(s32[1,100]{1,0:T(1,128)} %param.10) | copy-start | bytes 1204
  0.7 12.6 %copy-start.1 = (bf16[64,256]{1,0:T(8,128)(2,1)S(1)}, bf16[64,256]{1,0:T(8,128)(2,1)}, u32[]{:S(2)}) copy-start(bf16[64,256]{1,0:T(8,128)(2,1)} %param.8) | copy-start | bytes 98308
  2.5 44.2 %all-to-all-start = ((bf16[32,64,256]{2,1,0:T(8,128)(2,1)}), bf16[32,64,256]{2,1,0:T(8,128)(2,1)S(1)}, u32[]{:S(2)}, u32[]{:S(2)}) async-start(bf16[32,64,256]{2,1,0:T(8,128)(2,1)} %broadcast_in_dim.11), calls=%async_computation | async-start | bytes 2097152 | tf_op jit(solution)/shard_map/all_to_all | solution.py:113
  47.6 10.7 %all-to-all-start.1 = ((bf16[4,16,3328]{2,1,0:T(8,128)(2,1)}), bf16[4,16,3328]{2,1,0:T(8,128)(2,1)}, u32[]{:S(2)}, u32[]{:S(2)}) async-start(bf16[4,16,3328]{2,1,0:T(8,128)(2,1)} %broadcast_in_dim.10), calls=%async_computation.1 | async-start | bytes 851968 | tf_op jit(solution)/shard_map/all_to_all | solution.py:134
  51.7 11.8 %copy-start = (bf16[256,2816]{1,0:T(8,128)(2,1)S(1)}, bf16[256,2816]{1,0:T(8,128)(2,1)}, u32[]{:S(2)}) copy-start(bf16[256,2816]{1,0:T(8,128)(2,1)} %refs_2_.1) | copy-start | bytes 4325380
  64.8 19.9 %all-to-all-start.2 = ((f32[128,1,128]{2,1,0:T(1,128)}), f32[128,1,128]{2,1,0:T(1,128)S(1)}, u32[]{:S(2)}, u32[]{:S(2)}) async-start(f32[128,1,128]{2,1,0:T(1,128)} %bitcast.10), calls=%async_computation.2 | async-start | bytes 131072 | tf_op jit(solution)/shard_map/all_to_all | solution.py:166

commit v7 on v5

--- a/solution.py
+++ b/solution.py
@@ -117,15 +117,19 @@
     extra = full_width // head + 1
     sent = jnp.concatenate(
         [
-            queries_now,
-            queries_prev.reshape(extra - 1, head),
-            listed.reshape(1, head),
-            jnp.zeros((-extra % 16, head), queries_now.dtype),
+            queries_now.reshape(-1, 16, head),
+            jnp.concatenate(
+                [
+                    queries_prev.reshape(extra - 1, head),
+                    listed.reshape(1, head),
+                    jnp.zeros((-extra % 16, head), queries_now.dtype),
+                ]
+            ).reshape(-1, 16, head),
         ]
     )
     orders = [around, around[::-1]]
     rings = [[z * cores + (z + ring) % cores for z in orders[ring]] for ring in range(cores)]
-    column = lax.all_gather(sent, PAIR, axis_index_groups=rings)
+    column = lax.all_gather(sent, PAIR, tiled=True, axis_index_groups=rings).reshape(depth, -1, head)
     asked = column[:, own_rows : own_rows + extra].reshape(depth, extra * head)
 
     asked = jnp.broadcast_to(asked[None], (ys,) + asked.shape)

time: 85.8 us -> 85.8 us (level)
  no operation moved by 1% of the time
where the time goes in v7:
time: 85.8 us; the launch traced here: 85.4 us
  blocking collectives  38.6 us (45%)
  starting transfers between devices  29 us (34%)
  waiting for transfers between devices  7.77 us (9%)
  Pallas kernels  5.45 us (6%)
  local copies, waits for them, and re-layouts  2.82 us (3%)
  between operations  1.43 us (2%)
    all_gather x1, blocking collectives, local(): lax.all_gather(sent, PAIR, tiled=True, axis_index_groups=rings)  33.3 us
    all_to_all x1, starting transfers between devices, local(): lax.all_to_all(merged, BACK, 0, 0, tiled=True, axis_index_groups=[groups])  14.3 us
    all_to_all x1, starting transfers between devices, local(): lax.all_to_all(jnp.broadcast_to(prefixes[None], (plane * lax.axis_size('x...  10.6 us
    all_gather x1, blocking collectives, local(): asked = lax.all_gather(asked, PAIR, tiled=True, axis_index_groups=pairs)  5.25 us
    all_to_all x1, waiting for transfers between devices, local(): lax.all_to_all(merged, BACK, 0, 0, tiled=True, axis_index_groups=[groups])  4.74 us
    all_to_all x1, starting transfers between devices, local(): lax.all_to_all(asked, 'y', 0, 0, tiled=True).reshape(-1, extra * head)  4.12 us
    pallas_call x1, Pallas kernels, local(): pl.pallas_call(lambda *refs: partial_lse(head ** (-0.5), own_rows, *refs)...  3.45 us
    all_to_all x1, waiting for transfers between devices, local(): lax.all_to_all(asked, 'y', 0, 0, tiled=True).reshape(-1, extra * head)  3.03 us
  transfers between devices with their start and end apart: 3, of which 2 were waited for; matrix products, arithmetic and copies ran while one was open for 1% of the time, Pallas kernels for 4%

profile of v7, /device:TPU:1, one launch (start us, length us, event | category | flops | bytes accessed | tf_op | source)
XLA Modules:
  0.0 85.4 jit_solution(9603731237029341482)
XLA Ops:
  0.6 0.0 copy-start.2
  0.6 0.0 copy-start.3
  0.7 0.0 copy-start.1
  0.7 1.9 %broadcast_in_dim.11 = bf16[32,64,256]{2,1,0:T(8,128)(2,1)} broadcast(bf16[64,256]{1,0:T(8,128)(2,1)} %param.6), dimensions={1,2} | broadcast | bytes 1081344 | tf_op jit(solution)/shard_map/broadcast_in_dim | solution.py:113
  2.5 10.6 %all-to-all-start = ((bf16[32,64,256]{2,1,0:T(8,128)(2,1)}), bf16[32,64,256]{2,1,0:T(8,128)(2,1)S(1)}, u32[]{:S(2)}, u32[]{:S(2)}) async-start(bf16[32,64,256]{2,1,0:T(8,128)(2,1)} %broadcast_in_dim.11), calls=%async_computation | async-start | bytes 2097152 | tf_op jit(solution)/shard_map/all_to_all | solution.py:112
  13.1 0.0 copy-done.2
  13.2 0.1 pad.25.clone
  13.2 0.0 copy-done.3
  13.3 0.1 maximum_bitcast_fusion
  13.4 0.0 copy-done.1
  13.4 33.3 %all_gather.6 = bf16[80,16,256]{2,1,0:T(8,128)(2,1)S(1)} all-gather(bf16[5,16,256]{2,1,0:T(8,128)(2,1)S(1)} %pad_maximum_fusion), channel_id=1, replica_groups={{256,292,320,356,384,420,448,484,0,36,64,100,128,164,192,228},{224,196,..., dimensions={0}, use_global_device_ids=true | all-gather | bytes 696320 | tf_op jit(solution)/shard_map/all_gather | solution.py:132
  46.8 0.0 all-to-all-done
  46.8 0.8 broadcast_in_dim.10
  47.6 4.1 %all-to-all-start.1 = ((bf16[4,16,3328]{2,1,0:T(8,128)(2,1)}), bf16[4,16,3328]{2,1,0:T(8,128)(2,1)}, u32[]{:S(2)}, u32[]{:S(2)}) async-start(bf16[4,16,3328]{2,1,0:T(8,128)(2,1)} %broadcast_in_dim.10), calls=%async_computation.1 | async-start | bytes 851968 | tf_op jit(solution)/shard_map/all_to_all | solution.py:137
  51.7 0.0 copy-start
  51.7 3.4 %partial_lse.1.refs_3_ = f32[16,128]{1,0:T(8,128)S(1)} custom-call(bf16[16,80,256]{2,1,0:T(8,128)(2,1)S(1)} %bitcast.42, bf16[2048,256]{1,0:T(8,128)(2,1)S(1)} %bitcast.39), custom_call_target="tpu_custom_call" | custom-call | flops 536870912 | bytes 2097152 | tf_op jit(solution)/shard_map/partial_lse/pallas_call | solution.py:142
  55.2 3.0 %all-to-all-done.1 = bf16[4,16,3328]{2,1,0:T(8,128)(2,1)} async-done(((bf16[4,16,3328]{2,1,0:T(8,128)(2,1)}), bf16[4,16,3328]{2,1,0:T(8,128)(2,1)}, u32[]{:S(2)}, u32[]{:S(2)}) %all-to-all-start.1) | async-done | bytes 426016 | tf_op jit(solution)/shard_map/all_to_all | solution.py:137
  58.2 5.3 %all_gather.7.refs_0_ = bf16[128,3328]{1,0:T(8,128)(2,1)S(1)} all-gather(bf16[64,3328]{1,0:T(8,128)(2,1)} %bitcast.10), channel_id=1, replica_groups={{0,4},{36,32},{64,68},{100,96},{128,132},{164,160},{192,196},{228,224},..., dimensions={0}, use_global_device_ids=true | all-gather | bytes 1277952 | tf_op jit(solution)/shard_map/all_gather | solution.py:139
  63.5 0.0 copy-done
  63.5 1.3 %listed_scores.1 = f32[128,128]{1,0:T(8,128)} custom-call(bf16[128,3328]{1,0:T(8,128)(2,1)S(1)} %all_gather.7.refs_0_, bf16[2048,256]{1,0:T(8,128)(2,1)S(1)} %bitcast.40, bf16[256,2816]{1,0:T(8,128)(2,1)S(1)} %copy-done, f32[16,128]{1,0:T(8,128)S(1)} %partial_lse.1.refs_3_), custom_call_target="tpu_custom_call" | custom-call | flops 201326592 | bytes 3145728 | tf_op jit(solution)/shard_map/listed_scores/pallas_call | solution.py:158
  64.8 14.3 %all-to-all-start.2 = ((f32[128,1,128]{2,1,0:T(1,128)}), f32[128,1,128]{2,1,0:T(1,128)S(1)}, u32[]{:S(2)}, u32[]{:S(2)}) async-start(f32[128,1,128]{2,1,0:T(1,128)} %bitcast.12), calls=%async_computation.2 | async-start | bytes 131072 | tf_op jit(solution)/shard_map/all_to_all | solution.py:169
  79.1 0.2 fusion.1
  80.0 4.7 %all-to-all-done.2 = f32[128,1,128]{2,1,0:T(1,128)S(1)} async-done(((f32[128,1,128]{2,1,0:T(1,128)}), f32[128,1,128]{2,1,0:T(1,128)S(1)}, u32[]{:S(2)}, u32[]{:S(2)}) %all-to-all-start.2) | async-done | bytes 65568 | tf_op jit(solution)/shard_map/all_to_all | solution.py:169
  84.7 0.7 finish.1
  (12 shorter events, 0.2 us)
Async XLA Ops:
  0.6 12.5 %copy-start.2 = (bf16[1,3072]{1,0:T(2,128)(2,1)S(1)}, bf16[1,3072]{1,0:T(2,128)(2,1)}, u32[]{:S(2)}) copy-start(bf16[1,3072]{1,0:T(2,128)(2,1)} %param.9) | copy-start | bytes 18436
  0.6 12.6 %copy-start.3 = (s32[1,100]{1,0:T(1,128)S(1)}, s32[1,100]{1,0:T(1,128)}, u32[]{:S(2)}) copy-start(s32[1,100]{1,0:T(1,128)} %param.10) | copy-start | bytes 1204
  0.7 12.7 %copy-start.1 = (bf16[64,256]{1,0:T(8,128)(2,1)S(1)}, bf16[64,256]{1,0:T(8,128)(2,1)}, u32[]{:S(2)}) copy-start(bf16[64,256]{1,0:T(8,128)(2,1)} %param.8) | copy-start | bytes 98308
  2.5 44.2 %all-to-all-start = ((bf16[32,64,256]{2,1,0:T(8,128)(2,1)}), bf16[32,64,256]{2,1,0:T(8,128)(2,1)S(1)}, u32[]{:S(2)}, u32[]{:S(2)}) async-start(bf16[32,64,256]{2,1,0:T(8,128)(2,1)} %broadcast_in_dim.11), calls=%async_computation | async-start | bytes 2097152 | tf_op jit(solution)/shard_map/all_to_all | solution.py:112
  47.6 10.7 %all-to-all-start.1 = ((bf16[4,16,3328]{2,1,0:T(8,128)(2,1)}), bf16[4,16,3328]{2,1,0:T(8,128)(2,1)}, u32[]{:S(2)}, u32[]{:S(2)}) async-start(bf16[4,16,3328]{2,1,0:T(8,128)(2,1)} %broadcast_in_dim.10), calls=%async_computation.1 | async-start | bytes 851968 | tf_op jit(solution)/shard_map/all_to_all | solution.py:137
  51.7 11.8 %copy-start = (bf16[256,2816]{1,0:T(8,128)(2,1)S(1)}, bf16[256,2816]{1,0:T(8,128)(2,1)}, u32[]{:S(2)}) copy-start(bf16[256,2816]{1,0:T(8,128)(2,1)} %refs_2_.1) | copy-start | bytes 4325380
  64.8 19.9 %all-to-all-start.2 = ((f32[128,1,128]{2,1,0:T(1,128)}), f32[128,1,128]{2,1,0:T(1,128)S(1)}, u32[]{:S(2)}, u32[]{:S(2)}) async-start(f32[128,1,128]{2,1,0:T(1,128)} %bitcast.12), calls=%async_computation.2 | async-start | bytes 131072 | tf_op jit(solution)/shard_map/all_to_all | solution.py:169

commit v8 on v6

--- a/solution.py
+++ b/solution.py
@@ -116,17 +116,13 @@
     ).reshape(-1, head)
 
     extra = full_width // head + 1
-    sent = jnp.concatenate(
-        [
-            queries_now,
-            queries_prev.reshape(extra - 1, head),
-            listed.reshape(1, head),
-            jnp.zeros((-extra % 16, head), queries_now.dtype),
-        ]
+    asking = jnp.concatenate(
+        [queries_prev.reshape(extra - 1, head), listed.reshape(1, head), jnp.zeros((-extra % 16, head), queries_now.dtype)]
     )
+    sent = jnp.concatenate([queries_now.reshape(-1, 16, head), asking.reshape(-1, 16, head)])
     orders = [around, around[::-1]]
     rings = [[z * cores + (z + ring) % cores for z in orders[ring]] for ring in range(cores)]
-    column = lax.all_gather(sent, PAIR, axis_index_groups=rings)
+    column = lax.all_gather(sent, PAIR, tiled=True, axis_index_groups=rings).reshape(depth, -1, head)
     asked = column[:, own_rows : own_rows + extra].reshape(depth, extra * head)
 
     asked = jnp.broadcast_to(asked[None], (ys,) + asked.shape)
@@ -146,7 +142,7 @@
         out_specs=pl.BlockSpec((depth, LANES), lambda i: (0, 0)),
         out_shape=jax.ShapeDtypeStruct((depth, LANES), jnp.float32),
         scratch_shapes=[pltpu.VMEM((passages.shape[0], step * own_rows), jnp.float32)],
-        compiler_params=pltpu.CompilerParams(vmem_limit_bytes=32 * 2**20),
+        compiler_params=pltpu.CompilerParams(vmem_limit_bytes=12 * 2**20),
         cost_estimate=pl.CostEstimate(flops=2 * 2**28, bytes_accessed=2 * 2**20, transcendentals=2**21),
         name="partial_lse",
     )(column, passages)
@@ -157,7 +153,7 @@
         in_specs=[vmem, vmem, vmem, vmem],
         out_specs=vmem,
         out_shape=jax.ShapeDtypeStruct((plane * depth, LANES), jnp.float32),
-        compiler_params=pltpu.CompilerParams(vmem_limit_bytes=32 * 2**20),
+        compiler_params=pltpu.CompilerParams(vmem_limit_bytes=12 * 2**20),
         cost_estimate=pl.CostEstimate(flops=2 * 128 * 256 * 3072, bytes_accessed=3 * 2**20, transcendentals=0),
         name="listed_scores",
     )(asked, passages, tails, parts)
@@ -178,7 +174,7 @@
             jax.ShapeDtypeStruct((1, own_rows), jnp.float32),
             jax.ShapeDtypeStruct((1, count), jnp.float32),
         ],
-        compiler_params=pltpu.CompilerParams(vmem_limit_bytes=32 * 2**20),
+        compiler_params=pltpu.CompilerParams(vmem_limit_bytes=12 * 2**20),
         name="finish",
     )(
         jnp.pad(row, (0, LANES - count)).reshape(1, LANES),

time: 85.8 us -> 85.7 us (level)
  no operation moved by 1% of the time
where the time goes in v8:
time: 85.7 us; the launch traced here: 85.3 us
  blocking collectives  38.6 us (45%)
  starting transfers between devices  29 us (34%)
  waiting for transfers between devices  7.77 us (9%)
  Pallas kernels  5.4 us (6%)
  local copies, waits for them, and re-layouts  2.82 us (3%)
  between operations  1.43 us (2%)
    all_gather x1, blocking collectives, local(): lax.all_gather(sent, PAIR, tiled=True, axis_index_groups=rings)  33.3 us
    all_to_all x1, starting transfers between devices, local(): lax.all_to_all(merged, BACK, 0, 0, tiled=True, axis_index_groups=[groups])  14.3 us
    all_to_all x1, starting transfers between devices, local(): lax.all_to_all(jnp.broadcast_to(prefixes[None], (plane * lax.axis_size('x...  10.6 us
    all_gather x1, blocking collectives, local(): asked = lax.all_gather(asked, PAIR, tiled=True, axis_index_groups=pairs)  5.25 us
    all_to_all x1, waiting for transfers between devices, local(): lax.all_to_all(merged, BACK, 0, 0, tiled=True, axis_index_groups=[groups])  4.74 us
    all_to_all x1, starting transfers between devices, local(): lax.all_to_all(asked, 'y', 0, 0, tiled=True).reshape(-1, extra * head)  4.12 us
    pallas_call x1, Pallas kernels, local(): pl.pallas_call(lambda *refs: partial_lse(head ** (-0.5), own_rows, *refs)...  3.45 us
    all_to_all x1, waiting for transfers between devices, local(): lax.all_to_all(asked, 'y', 0, 0, tiled=True).reshape(-1, extra * head)  3.03 us
  transfers between devices with their start and end apart: 3, of which 2 were waited for; matrix products, arithmetic and copies ran while one was open for 1% of the time, Pallas kernels for 4%

profile of v8, /device:TPU:1, one launch (start us, length us, event | category | flops | bytes accessed | tf_op | source)
XLA Modules:
  0.0 85.3 jit_solution(12991202712567081366)
XLA Ops:
  0.6 0.0 copy-start.2
  0.6 0.0 copy-start.3
  0.7 0.0 copy-start.1
  0.7 1.9 %broadcast_in_dim.11 = bf16[32,64,256]{2,1,0:T(8,128)(2,1)} broadcast(bf16[64,256]{1,0:T(8,128)(2,1)} %param.6), dimensions={1,2} | broadcast | bytes 1081344 | tf_op jit(solution)/shard_map/broadcast_in_dim | solution.py:114
  2.5 10.6 %all-to-all-start = ((bf16[32,64,256]{2,1,0:T(8,128)(2,1)}), bf16[32,64,256]{2,1,0:T(8,128)(2,1)S(1)}, u32[]{:S(2)}, u32[]{:S(2)}) async-start(bf16[32,64,256]{2,1,0:T(8,128)(2,1)} %broadcast_in_dim.11), calls=%async_computation | async-start | bytes 2097152 | tf_op jit(solution)/shard_map/all_to_all | solution.py:113
  13.1 0.0 copy-done.2
  13.2 0.1 pad.25.clone
  13.2 0.0 copy-done.3
  13.3 0.1 maximum_bitcast_fusion
  13.4 0.0 copy-done.1
  13.4 33.3 %all_gather.6 = bf16[80,16,256]{2,1,0:T(8,128)(2,1)S(1)} all-gather(bf16[5,16,256]{2,1,0:T(8,128)(2,1)S(1)} %pad_maximum_fusion), channel_id=1, replica_groups={{256,292,320,356,384,420,448,484,0,36,64,100,128,164,192,228},{224,196,..., dimensions={0}, use_global_device_ids=true | all-gather | bytes 696320 | tf_op jit(solution)/shard_map/all_gather | solution.py:125
  46.8 0.0 all-to-all-done
  46.8 0.8 broadcast_in_dim.10
  47.6 4.1 %all-to-all-start.1 = ((bf16[4,16,3328]{2,1,0:T(8,128)(2,1)}), bf16[4,16,3328]{2,1,0:T(8,128)(2,1)}, u32[]{:S(2)}, u32[]{:S(2)}) async-start(bf16[4,16,3328]{2,1,0:T(8,128)(2,1)} %broadcast_in_dim.10), calls=%async_computation.1 | async-start | bytes 851968 | tf_op jit(solution)/shard_map/all_to_all | solution.py:130
  51.7 0.0 copy-start
  51.7 3.4 %partial_lse.1.refs_3_ = f32[16,128]{1,0:T(8,128)S(1)} custom-call(bf16[16,80,256]{2,1,0:T(8,128)(2,1)S(1)} %bitcast.44, bf16[2048,256]{1,0:T(8,128)(2,1)S(1)} %bitcast.41), custom_call_target="tpu_custom_call" | custom-call | flops 536870912 | bytes 2097152 | tf_op jit(solution)/shard_map/partial_lse/pallas_call | solution.py:135
  55.2 3.0 %all-to-all-done.1 = bf16[4,16,3328]{2,1,0:T(8,128)(2,1)} async-done(((bf16[4,16,3328]{2,1,0:T(8,128)(2,1)}), bf16[4,16,3328]{2,1,0:T(8,128)(2,1)}, u32[]{:S(2)}, u32[]{:S(2)}) %all-to-all-start.1) | async-done | bytes 426016 | tf_op jit(solution)/shard_map/all_to_all | solution.py:130
  58.2 5.3 %all_gather.7.refs_0_ = bf16[128,3328]{1,0:T(8,128)(2,1)S(1)} all-gather(bf16[64,3328]{1,0:T(8,128)(2,1)} %bitcast.10), channel_id=1, replica_groups={{0,4},{36,32},{64,68},{100,96},{128,132},{164,160},{192,196},{228,224},..., dimensions={0}, use_global_device_ids=true | all-gather | bytes 1277952 | tf_op jit(solution)/shard_map/all_gather | solution.py:132
  63.5 0.0 copy-done
  63.5 1.3 %listed_scores.1 = f32[128,128]{1,0:T(8,128)} custom-call(bf16[128,3328]{1,0:T(8,128)(2,1)S(1)} %all_gather.7.refs_0_, bf16[2048,256]{1,0:T(8,128)(2,1)S(1)} %bitcast.42, bf16[256,2816]{1,0:T(8,128)(2,1)S(1)} %copy-done, f32[16,128]{1,0:T(8,128)S(1)} %partial_lse.1.refs_3_), custom_call_target="tpu_custom_call" | custom-call | flops 201326592 | bytes 3145728 | tf_op jit(solution)/shard_map/listed_scores/pallas_call | solution.py:151
  64.8 14.3 %all-to-all-start.2 = ((f32[128,1,128]{2,1,0:T(1,128)}), f32[128,1,128]{2,1,0:T(1,128)S(1)}, u32[]{:S(2)}, u32[]{:S(2)}) async-start(f32[128,1,128]{2,1,0:T(1,128)} %bitcast.12), calls=%async_computation.2 | async-start | bytes 131072 | tf_op jit(solution)/shard_map/all_to_all | solution.py:162
  79.1 0.2 fusion.1
  79.9 4.7 %all-to-all-done.2 = f32[128,1,128]{2,1,0:T(1,128)S(1)} async-done(((f32[128,1,128]{2,1,0:T(1,128)}), f32[128,1,128]{2,1,0:T(1,128)S(1)}, u32[]{:S(2)}, u32[]{:S(2)}) %all-to-all-start.2) | async-done | bytes 65568 | tf_op jit(solution)/shard_map/all_to_all | solution.py:162
  84.7 0.7 finish.1
  (12 shorter events, 0.2 us)
Async XLA Ops:
  0.6 12.5 %copy-start.2 = (bf16[1,3072]{1,0:T(2,128)(2,1)S(1)}, bf16[1,3072]{1,0:T(2,128)(2,1)}, u32[]{:S(2)}) copy-start(bf16[1,3072]{1,0:T(2,128)(2,1)} %param.9) | copy-start | bytes 18436
  0.6 12.6 %copy-start.3 = (s32[1,100]{1,0:T(1,128)S(1)}, s32[1,100]{1,0:T(1,128)}, u32[]{:S(2)}) copy-start(s32[1,100]{1,0:T(1,128)} %param.10) | copy-start | bytes 1204
  0.7 12.7 %copy-start.1 = (bf16[64,256]{1,0:T(8,128)(2,1)S(1)}, bf16[64,256]{1,0:T(8,128)(2,1)}, u32[]{:S(2)}) copy-start(bf16[64,256]{1,0:T(8,128)(2,1)} %param.8) | copy-start | bytes 98308
  2.5 44.2 %all-to-all-start = ((bf16[32,64,256]{2,1,0:T(8,128)(2,1)}), bf16[32,64,256]{2,1,0:T(8,128)(2,1)S(1)}, u32[]{:S(2)}, u32[]{:S(2)}) async-start(bf16[32,64,256]{2,1,0:T(8,128)(2,1)} %broadcast_in_dim.11), calls=%async_computation | async-start | bytes 2097152 | tf_op jit(solution)/shard_map/all_to_all | solution.py:113
  47.6 10.7 %all-to-all-start.1 = ((bf16[4,16,3328]{2,1,0:T(8,128)(2,1)}), bf16[4,16,3328]{2,1,0:T(8,128)(2,1)}, u32[]{:S(2)}, u32[]{:S(2)}) async-start(bf16[4,16,3328]{2,1,0:T(8,128)(2,1)} %broadcast_in_dim.10), calls=%async_computation.1 | async-start | bytes 851968 | tf_op jit(solution)/shard_map/all_to_all | solution.py:130
  51.7 11.8 %copy-start = (bf16[256,2816]{1,0:T(8,128)(2,1)S(1)}, bf16[256,2816]{1,0:T(8,128)(2,1)}, u32[]{:S(2)}) copy-start(bf16[256,2816]{1,0:T(8,128)(2,1)} %refs_2_.1) | copy-start | bytes 4325380
  64.8 19.9 %all-to-all-start.2 = ((f32[128,1,128]{2,1,0:T(1,128)}), f32[128,1,128]{2,1,0:T(1,128)S(1)}, u32[]{:S(2)}, u32[]{:S(2)}) async-start(f32[128,1,128]{2,1,0:T(1,128)} %bitcast.12), calls=%async_computation.2 | async-start | bytes 131072 | tf_op jit(solution)/shard_map/all_to_all | solution.py:162

commit v9 on v5

--- a/solution.py
+++ b/solution.py
@@ -99,7 +99,7 @@
     shard_rows = tails.shape[0]
     full_width = queries_prev.shape[1]
     plane = ys * cores
-    turn = depth // 2
+    turn = 5 * depth // 8
     around = [(i + turn) % depth for i in range(depth)]
 
     ids = candidates.reshape(-1)
@@ -165,7 +165,7 @@
     back = lax.all_to_all(merged, BACK, 0, 0, tiled=True, axis_index_groups=[groups])
 
     far = shard // plane
-    ring, at = (shard + far) % cores, (far + turn) % depth
+    ring, at = (shard + far) % cores, (far - turn) % depth
     row = (ring * ys + shard // cores % ys) * depth + jnp.where(ring == 0, at, depth - 1 - at)
     before = jnp.arange(count)[:, None] > jnp.arange(count)[None, :]
     second = jnp.any((shard[:, None] == shard[None, :]) & before, axis=1).astype(jnp.int32)

time: 85.8 us -> 86 us (level)
  waiting for transfers between devices: 7.77 us -> 9.43 us
  starting transfers between devices: 29 us -> 27.5 us
    all_to_all x1, waiting for transfers between devices: 4.74 us -> 6.39 us  [local(): lax.all_to_all(merged, BACK, 0, 0, tiled=True, axis_index_groups=[groups])]
    all_to_all x1, starting transfers between devices: 14.3 us -> 12.8 us  [local(): lax.all_to_all(merged, BACK, 0, 0, tiled=True, axis_index_groups=[groups])]
where the time goes in v9:
time: 86 us; the launch traced here: 85.6 us
  blocking collectives  38.6 us (45%)
  starting transfers between devices  27.5 us (32%)
  waiting for transfers between devices  9.43 us (11%)
  Pallas kernels  5.45 us (6%)
  local copies, waits for them, and re-layouts  2.82 us (3%)
  between operations  1.44 us (2%)
    all_gather x1, blocking collectives, local(): column = lax.all_gather(sent, PAIR, axis_index_groups=rings)  33.3 us
    all_to_all x1, starting transfers between devices, local(): lax.all_to_all(merged, BACK, 0, 0, tiled=True, axis_index_groups=[groups])  12.8 us
    all_to_all x1, starting transfers between devices, local(): lax.all_to_all(jnp.broadcast_to(prefixes[None], (plane * lax.axis_size('x...  10.6 us
    all_to_all x1, waiting for transfers between devices, local(): lax.all_to_all(merged, BACK, 0, 0, tiled=True, axis_index_groups=[groups])  6.39 us
    all_gather x1, blocking collectives, local(): asked = lax.all_gather(asked, PAIR, tiled=True, axis_index_groups=pairs)  5.25 us
    all_to_all x1, starting transfers between devices, local(): lax.all_to_all(asked, 'y', 0, 0, tiled=True).reshape(-1, extra * head)  4.12 us
    pallas_call x1, Pallas kernels, local(): pl.pallas_call(lambda *refs: partial_lse(head ** (-0.5), own_rows, *refs)...  3.45 us
    all_to_all x1, waiting for transfers between devices, local(): lax.all_to_all(asked, 'y', 0, 0, tiled=True).reshape(-1, extra * head)  3.03 us
  transfers between devices with their start and end apart: 3, of which 2 were waited for; matrix products, arithmetic and copies ran while one was open for 1% of the time, Pallas kernels for 4%

profile of v9, /device:TPU:1, one launch (start us, length us, event | category | flops | bytes accessed | tf_op | source)
XLA Modules:
  0.0 85.6 jit_solution(16502995125269703067)
XLA Ops:
  0.6 0.0 copy-start.2
  0.6 0.0 copy-start.3
  0.7 0.0 copy-start.1
  0.7 1.9 %broadcast_in_dim.11 = bf16[32,64,256]{2,1,0:T(8,128)(2,1)} broadcast(bf16[64,256]{1,0:T(8,128)(2,1)} %param.6), dimensions={1,2} | broadcast | bytes 1081344 | tf_op jit(solution)/shard_map/broadcast_in_dim | solution.py:113
  2.5 10.6 %all-to-all-start = ((bf16[32,64,256]{2,1,0:T(8,128)(2,1)}), bf16[32,64,256]{2,1,0:T(8,128)(2,1)S(1)}, u32[]{:S(2)}, u32[]{:S(2)}) async-start(bf16[32,64,256]{2,1,0:T(8,128)(2,1)} %broadcast_in_dim.11), calls=%async_computation | async-start | bytes 2097152 | tf_op jit(solution)/shard_map/all_to_all | solution.py:112
  13.1 0.0 copy-done.2
  13.2 0.1 pad.24.clone
  13.2 0.0 copy-done.3
  13.3 0.0 copy-done.1
  13.3 0.1 maximum_maximum_fusion
  13.4 33.3 %all-gather = bf16[1280,256]{1,0:T(8,128)(2,1)S(1)} all-gather(bf16[80,256]{1,0:T(8,128)(2,1)S(1)} %maximum_maximum_fusion), channel_id=2, replica_groups={{320,356,384,420,448,484,0,36,64,100,128,164,192,228,256,292},{288,260,..., dimensions={0}, use_global_device_ids=true | all-gather | bytes 696320 | tf_op jit(solution)/shard_map/all_gather | solution.py:128
  46.8 0.0 all-to-all-done
  46.8 0.8 broadcast_in_dim.10
  47.6 4.1 %all-to-all-start.1 = ((bf16[4,16,3328]{2,1,0:T(8,128)(2,1)}), bf16[4,16,3328]{2,1,0:T(8,128)(2,1)}, u32[]{:S(2)}, u32[]{:S(2)}) async-start(bf16[4,16,3328]{2,1,0:T(8,128)(2,1)} %broadcast_in_dim.10), calls=%async_computation.1 | async-start | bytes 851968 | tf_op jit(solution)/shard_map/all_to_all | solution.py:133
  51.7 0.0 copy-start
  51.7 3.4 %partial_lse.1.refs_3_ = f32[16,128]{1,0:T(8,128)S(1)} custom-call(bf16[16,80,256]{2,1,0:T(8,128)(2,1)S(1)} %bitcast.39, bf16[2048,256]{1,0:T(8,128)(2,1)S(1)} %bitcast.36), custom_call_target="tpu_custom_call" | custom-call | flops 536870912 | bytes 2097152 | tf_op jit(solution)/shard_map/partial_lse/pallas_call | solution.py:138
  55.2 3.0 %all-to-all-done.1 = bf16[4,16,3328]{2,1,0:T(8,128)(2,1)} async-done(((bf16[4,16,3328]{2,1,0:T(8,128)(2,1)}), bf16[4,16,3328]{2,1,0:T(8,128)(2,1)}, u32[]{:S(2)}, u32[]{:S(2)}) %all-to-all-start.1) | async-done | bytes 426016 | tf_op jit(solution)/shard_map/all_to_all | solution.py:133
  58.2 5.3 %all_gather.11.refs_0_ = bf16[128,3328]{1,0:T(8,128)(2,1)S(1)} all-gather(bf16[64,3328]{1,0:T(8,128)(2,1)} %bitcast.8), channel_id=1, replica_groups={{0,4},{36,32},{64,68},{100,96},{128,132},{164,160},{192,196},{228,224},..., dimensions={0}, use_global_device_ids=true | all-gather | bytes 1277952 | tf_op jit(solution)/shard_map/all_gather | solution.py:135
  63.5 0.0 copy-done
  63.5 1.3 %listed_scores.1 = f32[128,128]{1,0:T(8,128)} custom-call(bf16[128,3328]{1,0:T(8,128)(2,1)S(1)} %all_gather.11.refs_0_, bf16[2048,256]{1,0:T(8,128)(2,1)S(1)} %bitcast.37, bf16[256,2816]{1,0:T(8,128)(2,1)S(1)} %copy-done, f32[16,128]{1,0:T(8,128)S(1)} %partial_lse.1.refs_3_), custom_call_target="tpu_custom_call" | custom-call | flops 201326592 | bytes 3145728 | tf_op jit(solution)/shard_map/listed_scores/pallas_call | solution.py:154
  64.8 12.8 %all-to-all-start.2 = ((f32[128,1,128]{2,1,0:T(1,128)}), f32[128,1,128]{2,1,0:T(1,128)S(1)}, u32[]{:S(2)}, u32[]{:S(2)}) async-start(f32[128,1,128]{2,1,0:T(1,128)} %bitcast.10), calls=%async_computation.2 | async-start | bytes 131072 | tf_op jit(solution)/shard_map/all_to_all | solution.py:165
  77.7 0.2 fusion.1
  78.5 6.4 %all-to-all-done.2 = f32[128,1,128]{2,1,0:T(1,128)S(1)} async-done(((f32[128,1,128]{2,1,0:T(1,128)}), f32[128,1,128]{2,1,0:T(1,128)S(1)}, u32[]{:S(2)}, u32[]{:S(2)}) %all-to-all-start.2) | async-done | bytes 65568 | tf_op jit(solution)/shard_map/all_to_all | solution.py:165
  84.9 0.7 finish.1
  (11 shorter events, 0.2 us)
Async XLA Ops:
  0.6 12.5 %copy-start.2 = (bf16[1,3072]{1,0:T(2,128)(2,1)S(1)}, bf16[1,3072]{1,0:T(2,128)(2,1)}, u32[]{:S(2)}) copy-start(bf16[1,3072]{1,0:T(2,128)(2,1)} %param.9) | copy-start | bytes 18436
  0.6 12.6 %copy-start.3 = (s32[1,100]{1,0:T(1,128)S(1)}, s32[1,100]{1,0:T(1,128)}, u32[]{:S(2)}) copy-start(s32[1,100]{1,0:T(1,128)} %param.10) | copy-start | bytes 1204
  0.7 12.6 %copy-start.1 = (bf16[64,256]{1,0:T(8,128)(2,1)S(1)}, bf16[64,256]{1,0:T(8,128)(2,1)}, u32[]{:S(2)}) copy-start(bf16[64,256]{1,0:T(8,128)(2,1)} %param.8) | copy-start | bytes 98308
  2.5 44.2 %all-to-all-start = ((bf16[32,64,256]{2,1,0:T(8,128)(2,1)}), bf16[32,64,256]{2,1,0:T(8,128)(2,1)S(1)}, u32[]{:S(2)}, u32[]{:S(2)}) async-start(bf16[32,64,256]{2,1,0:T(8,128)(2,1)} %broadcast_in_dim.11), calls=%async_computation | async-start | bytes 2097152 | tf_op jit(solution)/shard_map/all_to_all | solution.py:112
  47.6 10.7 %all-to-all-start.1 = ((bf16[4,16,3328]{2,1,0:T(8,128)(2,1)}), bf16[4,16,3328]{2,1,0:T(8,128)(2,1)}, u32[]{:S(2)}, u32[]{:S(2)}) async-start(bf16[4,16,3328]{2,1,0:T(8,128)(2,1)} %broadcast_in_dim.10), calls=%async_computation.1 | async-start | bytes 851968 | tf_op jit(solution)/shard_map/all_to_all | solution.py:133
  51.7 11.8 %copy-start = (bf16[256,2816]{1,0:T(8,128)(2,1)S(1)}, bf16[256,2816]{1,0:T(8,128)(2,1)}, u32[]{:S(2)}) copy-start(bf16[256,2816]{1,0:T(8,128)(2,1)} %refs_2_.1) | copy-start | bytes 4325380
  64.8 20.1 %all-to-all-start.2 = ((f32[128,1,128]{2,1,0:T(1,128)}), f32[128,1,128]{2,1,0:T(1,128)S(1)}, u32[]{:S(2)}, u32[]{:S(2)}) async-start(f32[128,1,128]{2,1,0:T(1,128)} %bitcast.10), calls=%async_computation.2 | async-start | bytes 131072 | tf_op jit(solution)/shard_map/all_to_all | solution.py:165
